TPU v7x, 256 devices: a whole 4x4x8 slice. The times are simulated.
256 devices in a mesh: seq: 8 (over y, core), head: 8 (over z), dp: 4 (over x).
Axes of the slice: x: 4, y: 4, z: 8, core: 2. Of those that a mesh axis runs over, the one named last changes fastest.
Arguments:
- queries: bfloat16 [9216, 8192], P(('dp', 'seq', 'head')), parts along dimension 0, may hold values from -20 to 20
- routed_keys: bfloat16 [9216, 1024], P(('dp', 'seq', 'head')), parts along dimension 0, may hold values from -4 to 4
- routed_values: bfloat16 [9216, 1024], P(('dp', 'seq', 'head')), parts along dimension 0, may hold values from -6 to 6
- output_gradient: bfloat16 [9216, 8192], P(('dp', 'seq', 'head')), parts along dimension 0, may hold values from -6 to 6
- positions: int32 [9216], P('dp'), parts along dimension 0, may hold values from 0 to 12287, as said below
- counts: int32 [32], P('dp'), parts along dimension 0, may hold values from 1 to 288, as said below
Outputs:
- attended: bfloat16 [9216, 8192], P(('dp', 'seq', 'head')), parts along dimension 0
- grad_query: bfloat16 [9216, 8192], P(('dp', 'seq', 'head')), parts along dimension 0
- key_state_gradient: bfloat16 [9216, 1024], P(('dp', 'seq', 'head')), parts along dimension 0
- value_state_gradient: bfloat16 [9216, 1024], P(('dp', 'seq', 'head')), parts along dimension 0
There are 4 independent parts, one for each index of `dp`. A program takes and returns all parts, laid end to end along the dimension named above; each array names one. Nothing has to cross between parts.
Inputs may be any that keep to these rules, and one draw needn't show every extreme that they name: `counts`: one sequence shard has exactly 288; every other shard has 96 or more. Within shard s all positions lie in s * 1536 to (s + 1) * 1536 - 1 and are distinct; the live slots of a shard are strictly increasing.
All inputs are finite; a program needn't handle non-finite values.
Results may differ from a plain program's by a relative error of at most 0.018.
Values may be sent and summed in bfloat16 or wider, within the bound.
A program may use at most 128 MiB of HBM per device.

v0:
```python
import jax
import jax.numpy as jnp
from jax import lax
from jax.sharding import PartitionSpec as P

QUERY_HEADS = 64
KEY_VALUE_HEADS = 8
HEAD_WIDTH = 128


ROPE_BASE = 500000.0


def rope_angles(position):
    inverse_freq = jnp.float32(ROPE_BASE) ** (
        -(jnp.arange(HEAD_WIDTH // 2, dtype=jnp.float32) * 2.0 / HEAD_WIDTH)
    )
    angle_table = position.astype(jnp.float32)[:, None] * inverse_freq[None, :]
    return (jnp.cos(angle_table), jnp.sin(angle_table))


def apply_rotary(vectors, cosine_table, sine_values):
    half_size = vectors.shape[-1] // 2
    lower_half = vectors[..., :half_size]
    upper_half = vectors[..., half_size:]
    cosine_table = cosine_table[:, None, :]
    sine_values = sine_values[:, None, :]
    return jnp.concatenate(
        [
            lower_half * cosine_table - upper_half * sine_values,
            upper_half * cosine_table + lower_half * sine_values,
        ],
        -1,
    )


def invert_rotary(vectors, cosine_table, sine_values):
    half_size = vectors.shape[-1] // 2
    lower_half = vectors[..., :half_size]
    upper_half = vectors[..., half_size:]
    cosine_table = cosine_table[:, None, :]
    sine_values = sine_values[:, None, :]
    return jnp.concatenate(
        [
            lower_half * cosine_table + upper_half * sine_values,
            upper_half * cosine_table - lower_half * sine_values,
        ],
        -1,
    )


def pick_rows(routed_count):
    for block_size in (1024, 768, 512, 384, 256):
        if routed_count % block_size == 0:
            return block_size
    return routed_count


def attend(query_in, grad_in, key_block, value_block, query_pos, query_live, key_pos, key_live):
    routed_count = query_in.shape[0]
    head_count = query_in.shape[1] // HEAD_WIDTH
    block_rows = pick_rows(routed_count)
    block_count = routed_count // block_rows
    score_scale = 1.0 / jnp.sqrt(jnp.float32(HEAD_WIDTH))
    query_blocks = query_in.reshape(block_count, block_rows, head_count, HEAD_WIDTH)
    grad_blocks = grad_in.reshape(block_count, block_rows, head_count, HEAD_WIDTH)
    pos_blocks = query_pos.reshape(block_count, block_rows)
    live_blocks = query_live.reshape(block_count, block_rows)

    def block_step(totals, pieces):
        query_part, grad_part, pos_part, live_part = pieces
        scores = (
            jnp.einsum("bhd,kd->hbk", query_part, key_block, preferred_element_type=jnp.float32)
            * score_scale
        )
        allowed = (key_pos[None, :] <= pos_part[:, None]) & key_live[None, :]
        scores = jnp.where(allowed[None], scores, -1e30)
        row_max = jnp.max(scores, -1, keepdims=True)
        weights = jnp.exp(scores - row_max)
        row_total = jnp.sum(weights, -1, keepdims=True)
        probs = weights / row_total * live_part.astype(jnp.float32)[None, :, None]
        probs_low = probs.astype(jnp.bfloat16)
        out_part = jnp.einsum(
            "hbk,kd->bhd", probs_low, value_block, preferred_element_type=jnp.float32
        ).astype(jnp.bfloat16)
        dprob = jnp.einsum(
            "bhd,kd->hbk", grad_part, value_block, preferred_element_type=jnp.float32
        )
        delta = jnp.sum(grad_part.astype(jnp.float32) * out_part.astype(jnp.float32), -1).T
        dscore = (probs * (dprob - delta[:, :, None])).astype(jnp.bfloat16)
        grad_q = (
            jnp.einsum("hbk,kd->bhd", dscore, key_block, preferred_element_type=jnp.float32)
            * score_scale
        )
        cosine_table, sine_values = rope_angles(pos_part)
        grad_q = invert_rotary(grad_q, cosine_table, sine_values).astype(jnp.bfloat16)
        key_total = (
            totals[0]
            + jnp.einsum("hbk,bhd->kd", dscore, query_part, preferred_element_type=jnp.float32)
            * score_scale
        )
        value_total = totals[1] + jnp.einsum(
            "hbk,bhd->kd", probs_low, grad_part, preferred_element_type=jnp.float32
        )
        totals = (key_total, value_total)
        return (totals, (out_part, grad_q, row_max[:, :, 0].T, row_total[:, :, 0].T, delta.T))

    zeros = jnp.zeros((routed_count, HEAD_WIDTH), jnp.float32)
    sums, stacked = lax.scan(
        block_step, (zeros, zeros), (query_blocks, grad_blocks, pos_blocks, live_blocks)
    )
    out_heads = stacked[0].reshape(routed_count, head_count * HEAD_WIDTH)
    grad_heads = stacked[1].reshape(routed_count, head_count * HEAD_WIDTH)
    row_stats = (
        stacked[2].reshape(routed_count, head_count),
        stacked[3].reshape(routed_count, head_count),
        stacked[4].reshape(routed_count, head_count),
    )
    return (out_heads, grad_heads, sums[0], sums[1], row_stats)


def shards(queries, routed_keys, routed_values, output_gradient, positions, counts):
    seq_count = lax.axis_size("seq")
    head_count = lax.axis_size("head")
    seq_index = lax.axis_index("seq")
    head_index = lax.axis_index("head")
    routed_count = positions.shape[0]
    capacity = routed_count // seq_count
    slot_rows = queries.shape[0]
    is_valid = jnp.arange(routed_count) % capacity < jnp.repeat(
        counts, capacity, total_repeat_length=routed_count
    )
    row_start = seq_index * capacity + head_index * slot_rows
    local_pos = lax.dynamic_slice_in_dim(positions, row_start, slot_rows)
    cosine_table, sine_values = rope_angles(local_pos)
    query_rotated = apply_rotary(
        queries.astype(jnp.float32).reshape(slot_rows, QUERY_HEADS, HEAD_WIDTH),
        cosine_table,
        sine_values,
    )
    query_rotated = query_rotated.astype(jnp.bfloat16).reshape(slot_rows, QUERY_HEADS * HEAD_WIDTH)
    key_rotated = apply_rotary(
        routed_keys.astype(jnp.float32).reshape(slot_rows, KEY_VALUE_HEADS, HEAD_WIDTH),
        cosine_table,
        sine_values,
    )
    key_rotated = key_rotated.astype(jnp.bfloat16).reshape(slot_rows, KEY_VALUE_HEADS * HEAD_WIDTH)
    key_split, value_split = (
        lax.all_to_all(key_rotated, "seq", split_axis=1, concat_axis=0, tiled=True),
        lax.all_to_all(routed_values, "seq", split_axis=1, concat_axis=0, tiled=True),
    )
    key_all, value_all = (
        lax.all_gather(key_split, "head", axis=0, tiled=True),
        lax.all_gather(value_split, "head", axis=0, tiled=True),
    )

    def by_head(vector):
        return (
            vector.reshape(seq_count, head_count, slot_rows)
            .transpose(1, 0, 2)
            .reshape(routed_count)
        )

    key_pos = by_head(positions)
    key_live = by_head(is_valid)
    query_in, grad_in = (
        lax.all_to_all(query_rotated, ("seq", "head"), split_axis=1, concat_axis=0, tiled=True),
        lax.all_to_all(output_gradient, ("seq", "head"), split_axis=1, concat_axis=0, tiled=True),
    )
    out_heads, grad_heads, key_grad, value_grad, row_stats = attend(
        query_in, grad_in, key_all, value_all, positions, is_valid, key_pos, key_live
    )
    key_summed, value_summed = (
        lax.psum_scatter(key_grad, "head", scatter_dimension=0, tiled=True),
        lax.psum_scatter(value_grad, "head", scatter_dimension=0, tiled=True),
    )
    key_unrotated, value_back = (
        lax.all_to_all(
            key_summed.astype(jnp.bfloat16), "seq", split_axis=0, concat_axis=1, tiled=True
        ).astype(key_summed.dtype),
        lax.all_to_all(
            value_summed.astype(jnp.bfloat16), "seq", split_axis=0, concat_axis=1, tiled=True
        ).astype(value_summed.dtype),
    )
    key_state_gradient = invert_rotary(
        key_unrotated.reshape(slot_rows, KEY_VALUE_HEADS, HEAD_WIDTH), cosine_table, sine_values
    )
    key_state_gradient = key_state_gradient.astype(jnp.bfloat16).reshape(
        slot_rows, KEY_VALUE_HEADS * HEAD_WIDTH
    )
    value_state_gradient = value_back.astype(jnp.bfloat16)
    attended, grad_query = (
        lax.all_to_all(out_heads, ("seq", "head"), split_axis=0, concat_axis=1, tiled=True),
        lax.all_to_all(grad_heads, ("seq", "head"), split_axis=0, concat_axis=1, tiled=True),
    )
    return (attended, grad_query, key_state_gradient, value_state_gradient)


def solution(mesh):
    in_specs = (
        P(("dp", "seq", "head"), None),
        P(("dp", "seq", "head"), None),
        P(("dp", "seq", "head"), None),
        P(("dp", "seq", "head"), None),
        P("dp"),
        P("dp"),
    )
    out_specs = (
        P(("dp", "seq", "head"), None),
        P(("dp", "seq", "head"), None),
        P(("dp", "seq", "head"), None),
        P(("dp", "seq", "head"), None),
    )
    return jax.shard_map(shards, mesh=mesh, in_specs=in_specs, out_specs=out_specs, check_vma=False)
```

profile of v0, /device:TPU:1, one launch (start us, length us, event | category | flops | bytes accessed | tf_op | source)
XLA Modules:
  0.0 350.6 jit_solution(14294630889271262309)
XLA Ops:
  10.0 6.5 %all-to-all-start.1 = ((bf16[36,8,128]{2,0,1:T(8,128)(2,1)}), bf16[36,8,128]{2,0,1:T(8,128)(2,1)S(1)}, u32[]{:S(2)}, u32[]{:S(2)}) async-start(bf16[36,8,128]{2,0,1:T(8,128)(2,1)} %copy.43), calls=%async_computation.1 | async-start | bytes 163840 | tf_op jit(solution)/shard_map/all_to_all | solution.py:149
  17.3 1.4 subtract_convert_fusion
  19.4 2.1 all-to-all-done.1
  21.5 4.1 %all-to-all-start.3 = ((bf16[36,8,128]{2,0,1:T(8,128)(2,1)}), bf16[36,8,128]{2,0,1:T(8,128)(2,1)S(1)}, u32[]{:S(2)}, u32[]{:S(2)}) async-start(bf16[36,8,128]{2,0,1:T(8,128)(2,1)} %copy.45), calls=%async_computation.3 | async-start | bytes 163840 | tf_op jit(solution)/shard_map/all_to_all | solution.py:150
  26.7 3.7 %all-to-all-done.3 = bf16[36,8,128]{2,0,1:T(8,128)(2,1)S(1)} async-done(((bf16[36,8,128]{2,0,1:T(8,128)(2,1)}), bf16[36,8,128]{2,0,1:T(8,128)(2,1)S(1)}, u32[]{:S(2)}, u32[]{:S(2)}) %all-to-all-start.3) | async-done | bytes 73760 | tf_op jit(solution)/shard_map/all_to_all | solution.py:150
  30.5 9.9 %all-to-all-start = ((bf16[36,64,128]{2,0,1:T(8,128)(2,1)}), bf16[36,64,128]{2,0,1:T(8,128)(2,1)S(1)}, u32[]{:S(2)}, u32[]{:S(2)}) async-start(bf16[36,64,128]{2,0,1:T(8,128)(2,1)} %pad_maximum_fusion.1), calls=%async_computation | async-start | bytes 1310720 | tf_op jit(solution)/shard_map/all_to_all | solution.py:167
  40.6 1.2 copy.44
  41.8 18.3 %all-to-all-done = bf16[36,64,128]{2,0,1:T(8,128)(2,1)S(1)} async-done(((bf16[36,64,128]{2,0,1:T(8,128)(2,1)}), bf16[36,64,128]{2,0,1:T(8,128)(2,1)S(1)}, u32[]{:S(2)}, u32[]{:S(2)}) %all-to-all-start) | async-done | bytes 589856 | tf_op jit(solution)/shard_map/all_to_all | solution.py:167
  60.2 6.6 %all-to-all-start.2 = ((bf16[36,64,128]{2,0,1:T(8,128)(2,1)}), bf16[36,64,128]{2,0,1:T(8,128)(2,1)S(1)}, u32[]{:S(2)}, u32[]{:S(2)}) async-start(bf16[36,64,128]{2,0,1:T(8,128)(2,1)} %copy.44), calls=%async_computation.2 | async-start | bytes 1310720 | tf_op jit(solution)/shard_map/all_to_all | solution.py:168
  67.7 5.8 %select_select_fusion.1 = s32[2304]{0:T(1024)S(1)} fusion(pred[2304]{0:T(1024)(128)(4,1)S(1)} %copy-done.6, pred[2304]{0:T(1024)(128)(4,1)S(1)} %copy-done.7, pred[2304]{0:T(1024)(128)(4,1)} %constant.227, pred[2304]{0:T(1024)(128)(4,1)} %constant.228, pred[2304]{0:T(1024)(128)(4,1)} %constant.229, pred[2304]{0:T(1024)(128)(4,1)} %constant.230, ...), kind=kLoop, calls=%fused_computation.73 | loop fusion | flops 16128 | bytes 25376 | tf_op jit(solution)/shard_map/jit(_take)/gather | solution.py:130
  73.7 27.3 %all_gather.6 = bf16[2304,128]{1,0:T(8,128)(2,1)} all-gather(bf16[288,128]{1,0:T(8,128)(2,1)S(1)} %all_to_all.104), channel_id=1, replica_groups=mesh['seq'=8,'head'=8,'dp'=4] {'head'}, dimensions={0}, use_global_device_ids=true | all-gather | bytes 663552 | tf_op jit(solution)/shard_map/all_gather | solution.py:153
  101.0 22.2 %all_gather.7 = bf16[2304,128]{1,0:T(8,128)(2,1)} all-gather(bf16[288,128]{1,0:T(8,128)(2,1)S(1)} %all_to_all.111), channel_id=1, replica_groups=mesh['seq'=8,'head'=8,'dp'=4] {'head'}, dimensions={0}, use_global_device_ids=true | all-gather | bytes 663552 | tf_op jit(solution)/shard_map/all_gather | solution.py:154
  125.1 108.5 %while.21 = (s32[]{:T(128)}, f32[2304,128]{1,0:T(8,128)}, f32[2304,128]{1,0:T(8,128)}, bf16[3,768,1,128]{3,1,0,2:T(8,128)(2,1)}, bf16[3,768,1,128]{3,1,0,2:T(8,1...) while((s32[]{:T(128)}, f32[2304,128]{1,0:T(8,128)}, ...), condition=%wide.wide.region_4.5_spmd.clone, body=%wide.wide.region_0.0_spmd.clone.sunk | while | flops 2747391744 | bytes 136147552 | solution.py:109
  125.1 5.8 %select_select_fusion.4 = s32[2304]{0:T(1024)S(1)} fusion(pred[2304]{0:T(1024)(128)(4,1)S(1)} %get-tuple-element.696, pred[2304]{0:T(1024)(128)(4,1)S(1)} %get-tuple-element.697, pred[2304]{0:T(1024)(128)(4,1)} %get-tuple-element.698, pred[2304]{0:T(1024)(128)(4,1)} %get-tuple-element.699, pred[2304]{0:T(1024)(128)(4,1)} %get-tuple-element.700, ...), kind=kLoop, calls=%fused_computation.49.clone.clone.1 | loop fusion | flops 16128 | bytes 25376 | tf_op jit(solution)/shard_map/jit(_take)/gather | solution.py:130
  131.2 3.1 fusion.104
  135.4 3.6 %divide_multiply_fusion.3 = f32[1,768,2304]{2,1,0:T(8,128)} fusion(f32[1,768,2304]{2,1,0:T(8,128)S(1)} %get-tuple-element.606, f32[768]{0:T(1024)S(1)} %fusion.105, f32[768]{0:T(1024)S(1)} %fusion.106, f32[768]{0:T(1024)S(1)} %get-tuple-element.607), kind=kLoop, calls=%fused_computation.6.clone.clone.1 | loop fusion | flops 5308416 | bytes 14164992 | tf_op jit(solution)/shard_map/while/body/eval_jaxpr/mul | solution.py:81
  140.2 5.2 %fusion.107 = (f32[768]{0:T(1024)S(1)}, bf16[768,128]{0,1:T(8,128)(2,1)}) fusion(bf16[1,768,1,128]{1,3,2,0:T(8,128)(2,1)S(1)} %copy.84, bf16[2304,128]{1,0:T(8,128)(2,1)} %get-tuple-element.685, f32[1,768,2304]{2,1,0:T(8,128)} %divide_multiply_fusion.3), kind=kOutput, calls=%fused_computation.22.clone.clone.1 | convolution fusion | flops 455245056 | bytes 8064000 | tf_op jit(solution)/shard_map/while/body/eval_jaxpr/hbk,kd->bhd/dot_general | solution.py:83
  145.4 2.2 fusion.108
  147.6 3.0 fusion.110
  153.5 4.3 %fusion.109 = f32[2304,128]{1,0:T(8,128)} fusion(bf16[768,2304]{1,0:T(8,128)(2,1)} %copy-done.1, f32[2304,128]{1,0:T(8,128)} %get-tuple-element.645, pred[]{:T(512)S(6)} %compare.17, bf16[3,768,1,128]{3,1,2,0:T(8,128)(2,1)} %get-tuple-element.681, s32[]{:T(128)} %get-tuple-element.644), kind=kOutput, calls=%fused_computation.12.clone.clone.1 | convolution fusion | flops 453869568 | bytes 6095361 | tf_op jit(solution)/shard_map/while/body/eval_jaxpr/hbk,bhd->kd/dot_general | solution.py:99
  157.9 2.2 convolution_add_fusion.3
  160.2 5.8 %select_select_fusion.4 = s32[2304]{0:T(1024)S(1)} fusion(pred[2304]{0:T(1024)(128)(4,1)S(1)} %get-tuple-element.696, pred[2304]{0:T(1024)(128)(4,1)S(1)} %get-tuple-element.697, pred[2304]{0:T(1024)(128)(4,1)} %get-tuple-element.698, pred[2304]{0:T(1024)(128)(4,1)} %get-tuple-element.699, pred[2304]{0:T(1024)(128)(4,1)} %get-tuple-element.700, ...), kind=kLoop, calls=%fused_computation.49.clone.clone.1 | loop fusion | flops 16128 | bytes 25376 | tf_op jit(solution)/shard_map/jit(_take)/gather | solution.py:130
  166.2 3.2 fusion.104
  170.5 3.6 %divide_multiply_fusion.3 = f32[1,768,2304]{2,1,0:T(8,128)} fusion(f32[1,768,2304]{2,1,0:T(8,128)S(1)} %get-tuple-element.606, f32[768]{0:T(1024)S(1)} %fusion.105, f32[768]{0:T(1024)S(1)} %fusion.106, f32[768]{0:T(1024)S(1)} %get-tuple-element.607), kind=kLoop, calls=%fused_computation.6.clone.clone.1 | loop fusion | flops 5308416 | bytes 14164992 | tf_op jit(solution)/shard_map/while/body/eval_jaxpr/mul | solution.py:81
  175.3 5.2 %fusion.107 = (f32[768]{0:T(1024)S(1)}, bf16[768,128]{0,1:T(8,128)(2,1)}) fusion(bf16[1,768,1,128]{1,3,2,0:T(8,128)(2,1)S(1)} %copy.84, bf16[2304,128]{1,0:T(8,128)(2,1)} %get-tuple-element.685, f32[1,768,2304]{2,1,0:T(8,128)} %divide_multiply_fusion.3), kind=kOutput, calls=%fused_computation.22.clone.clone.1 | convolution fusion | flops 455245056 | bytes 8064000 | tf_op jit(solution)/shard_map/while/body/eval_jaxpr/hbk,kd->bhd/dot_general | solution.py:83
  180.5 2.2 fusion.108
  182.7 3.0 fusion.110
  188.6 4.7 %fusion.109 = f32[2304,128]{1,0:T(8,128)} fusion(bf16[768,2304]{1,0:T(8,128)(2,1)} %copy-done.1, f32[2304,128]{1,0:T(8,128)} %get-tuple-element.645, pred[]{:T(512)S(6)} %compare.17, bf16[3,768,1,128]{3,1,2,0:T(8,128)(2,1)} %get-tuple-element.681, s32[]{:T(128)} %get-tuple-element.644), kind=kOutput, calls=%fused_computation.12.clone.clone.1 | convolution fusion | flops 453869568 | bytes 6095361 | tf_op jit(solution)/shard_map/while/body/eval_jaxpr/hbk,bhd->kd/dot_general | solution.py:99
  193.3 3.5 convolution_add_fusion.3
  196.9 5.8 %select_select_fusion.4 = s32[2304]{0:T(1024)S(1)} fusion(pred[2304]{0:T(1024)(128)(4,1)S(1)} %get-tuple-element.696, pred[2304]{0:T(1024)(128)(4,1)S(1)} %get-tuple-element.697, pred[2304]{0:T(1024)(128)(4,1)} %get-tuple-element.698, pred[2304]{0:T(1024)(128)(4,1)} %get-tuple-element.699, pred[2304]{0:T(1024)(128)(4,1)} %get-tuple-element.700, ...), kind=kLoop, calls=%fused_computation.49.clone.clone.1 | loop fusion | flops 16128 | bytes 25376 | tf_op jit(solution)/shard_map/jit(_take)/gather | solution.py:130
  202.9 3.1 fusion.104
  207.2 3.6 %divide_multiply_fusion.3 = f32[1,768,2304]{2,1,0:T(8,128)} fusion(f32[1,768,2304]{2,1,0:T(8,128)S(1)} %get-tuple-element.606, f32[768]{0:T(1024)S(1)} %fusion.105, f32[768]{0:T(1024)S(1)} %fusion.106, f32[768]{0:T(1024)S(1)} %get-tuple-element.607), kind=kLoop, calls=%fused_computation.6.clone.clone.1 | loop fusion | flops 5308416 | bytes 14164992 | tf_op jit(solution)/shard_map/while/body/eval_jaxpr/mul | solution.py:81
  212.0 5.2 %fusion.107 = (f32[768]{0:T(1024)S(1)}, bf16[768,128]{0,1:T(8,128)(2,1)}) fusion(bf16[1,768,1,128]{1,3,2,0:T(8,128)(2,1)S(1)} %copy.84, bf16[2304,128]{1,0:T(8,128)(2,1)} %get-tuple-element.685, f32[1,768,2304]{2,1,0:T(8,128)} %divide_multiply_fusion.3), kind=kOutput, calls=%fused_computation.22.clone.clone.1 | convolution fusion | flops 455245056 | bytes 8064000 | tf_op jit(solution)/shard_map/while/body/eval_jaxpr/hbk,kd->bhd/dot_general | solution.py:83
  217.2 2.2 fusion.108
  219.4 3.0 fusion.110
  225.3 4.7 %fusion.109 = f32[2304,128]{1,0:T(8,128)} fusion(bf16[768,2304]{1,0:T(8,128)(2,1)} %copy-done.1, f32[2304,128]{1,0:T(8,128)} %get-tuple-element.645, pred[]{:T(512)S(6)} %compare.17, bf16[3,768,1,128]{3,1,2,0:T(8,128)(2,1)} %get-tuple-element.681, s32[]{:T(128)} %get-tuple-element.644), kind=kOutput, calls=%fused_computation.12.clone.clone.1 | convolution fusion | flops 453869568 | bytes 6095361 | tf_op jit(solution)/shard_map/while/body/eval_jaxpr/hbk,bhd->kd/dot_general | solution.py:99
  230.0 3.5 convolution_add_fusion.3
  233.6 2.0 all_to_all.112
  235.6 19.8 %all-to-all-start.4 = ((bf16[64,36,128]{2,1,0:T(8,128)(2,1)}), bf16[64,36,128]{2,1,0:T(8,128)(2,1)S(1)}, u32[]{:S(2)}, u32[]{:S(2)}) async-start(bf16[64,36,128]{2,1,0:T(8,128)(2,1)} %all_to_all.112), calls=%async_computation.4 | async-start | bytes 1310720 | tf_op jit(solution)/shard_map/all_to_all | solution.py:193
  257.1 25.4 %all-to-all-done.4 = bf16[64,36,128]{2,1,0:T(8,128)(2,1)S(1)} async-done(((bf16[64,36,128]{2,1,0:T(8,128)(2,1)}), bf16[64,36,128]{2,1,0:T(8,128)(2,1)S(1)}, u32[]{:S(2)}, u32[]{:S(2)}) %all-to-all-start.4) | async-done | bytes 589856 | tf_op jit(solution)/shard_map/all_to_all | solution.py:193
  282.5 6.3 %all-to-all-start.5 = ((bf16[64,36,128]{2,1,0:T(8,128)(2,1)}), bf16[64,36,128]{2,1,0:T(8,128)(2,1)S(1)}, u32[]{:S(2)}, u32[]{:S(2)}) async-start(bf16[64,36,128]{2,1,0:T(8,128)(2,1)} %all_to_all.116), calls=%async_computation.5 | async-start | bytes 1310720 | tf_op jit(solution)/shard_map/all_to_all | solution.py:194
  290.4 18.2 %all-to-all-done.5 = bf16[64,36,128]{2,1,0:T(8,128)(2,1)S(1)} async-done(((bf16[64,36,128]{2,1,0:T(8,128)(2,1)}), bf16[64,36,128]{2,1,0:T(8,128)(2,1)S(1)}, u32[]{:S(2)}, u32[]{:S(2)}) %all-to-all-start.5) | async-done | bytes 589856 | tf_op jit(solution)/shard_map/all_to_all | solution.py:194
  308.7 5.4 %all-to-all-start.6 = ((bf16[8,36,128]{2,1,0:T(8,128)(2,1)}), bf16[8,36,128]{2,1,0:T(8,128)(2,1)S(1)}, u32[]{:S(2)}, u32[]{:S(2)}) async-start(bf16[8,36,128]{2,1,0:T(8,128)(2,1)} %all_to_all.120), calls=%async_computation.7 | async-start | bytes 163840 | tf_op jit(solution)/shard_map/all_to_all | solution.py:178
  314.3 1.3 copy.66
  315.8 1.3 copy.67
  317.1 10.5 %reduce-scatter.5.cloned.1.call-done = f32[288,128]{1,0:T(8,128)} async-done(((f32[2304,128]{1,0:T(8,128)}), f32[288,128]{1,0:T(8,128)}) %reduce-scatter.5.cloned.1.call-update) | async-done | bytes 147472 | tf_op jit(solution)/shard_map/reduce_scatter | solution.py:175
  329.2 9.0 %all-to-all-start.7 = ((bf16[8,36,128]{2,1,0:T(8,128)(2,1)}), bf16[8,36,128]{2,1,0:T(8,128)(2,1)S(1)}, u32[]{:S(2)}, u32[]{:S(2)}) async-start(bf16[8,36,128]{2,1,0:T(8,128)(2,1)} %all_to_all.122), calls=%async_computation.9 | async-start | bytes 163840 | tf_op jit(solution)/shard_map/all_to_all | solution.py:181
  339.1 4.0 %all-to-all-done.7 = bf16[8,36,128]{2,1,0:T(8,128)(2,1)S(1)} async-done(((bf16[8,36,128]{2,1,0:T(8,128)(2,1)}), bf16[8,36,128]{2,1,0:T(8,128)(2,1)S(1)}, u32[]{:S(2)}, u32[]{:S(2)}) %all-to-all-start.7) | async-done | bytes 73760 | tf_op jit(solution)/shard_map/all_to_all | solution.py:181
  (186 shorter events, 31.5 us)
Async XLA Ops:
  7.2 9.4 %copy-start.3 = (bf16[36,8192]{1,0:T(8,128)(2,1)S(1)}, bf16[36,8192]{1,0:T(8,128)(2,1)}, u32[]{:S(2)}) copy-start(bf16[36,8192]{1,0:T(8,128)(2,1)} %param.10) | copy-start | bytes 1769476
  10.0 11.4 %all-to-all-start.1 = ((bf16[36,8,128]{2,0,1:T(8,128)(2,1)}), bf16[36,8,128]{2,0,1:T(8,128)(2,1)S(1)}, u32[]{:S(2)}, u32[]{:S(2)}) async-start(bf16[36,8,128]{2,0,1:T(8,128)(2,1)} %copy.43), calls=%async_computation.1 | async-start | bytes 163840 | tf_op jit(solution)/shard_map/all_to_all | solution.py:149
  18.7 21.6 %copy-start.2 = (bf16[36,8192]{1,0:T(8,128)(2,1)S(1)}, bf16[36,8192]{1,0:T(8,128)(2,1)}, u32[]{:S(2)}) copy-start(bf16[36,8192]{1,0:T(8,128)(2,1)} %param.13) | copy-start | bytes 1769476
  21.5 9.0 %all-to-all-start.3 = ((bf16[36,8,128]{2,0,1:T(8,128)(2,1)}), bf16[36,8,128]{2,0,1:T(8,128)(2,1)S(1)}, u32[]{:S(2)}, u32[]{:S(2)}) async-start(bf16[36,8,128]{2,0,1:T(8,128)(2,1)} %copy.45), calls=%async_computation.3 | async-start | bytes 163840 | tf_op jit(solution)/shard_map/all_to_all | solution.py:150
  30.5 29.7 %all-to-all-start = ((bf16[36,64,128]{2,0,1:T(8,128)(2,1)}), bf16[36,64,128]{2,0,1:T(8,128)(2,1)S(1)}, u32[]{:S(2)}, u32[]{:S(2)}) async-start(bf16[36,64,128]{2,0,1:T(8,128)(2,1)} %pad_maximum_fusion.1), calls=%async_computation | async-start | bytes 1310720 | tf_op jit(solution)/shard_map/all_to_all | solution.py:167
  40.5 26.4 %copy-start.13 = (s32[2304]{0:T(1024)S(1)}, s32[2304]{0:T(1024)}, u32[]{:S(2)}) copy-start(s32[2304]{0:T(1024)} %param.14) | copy-start | bytes 27652
  40.5 26.5 %copy-start.14 = (s32[8]{0:T(128)S(1)}, s32[8]{0:T(128)}, u32[]{:S(2)}) copy-start(s32[8]{0:T(128)} %param.15) | copy-start | bytes 100
  40.5 27.2 %copy-start.6 = (pred[2304]{0:T(1024)(128)(4,1)S(1)}, pred[2304]{0:T(1024)(128)(4,1)}, u32[]{:S(2)}) copy-start(pred[2304]{0:T(1024)(128)(4,1)} %constant.225) | copy-start | bytes 6916
  40.5 27.2 %copy-start.7 = (pred[2304]{0:T(1024)(128)(4,1)S(1)}, pred[2304]{0:T(1024)(128)(4,1)}, u32[]{:S(2)}) copy-start(pred[2304]{0:T(1024)(128)(4,1)} %constant.226) | copy-start | bytes 6916
  60.2 64.0 %all-to-all-start.2 = ((bf16[36,64,128]{2,0,1:T(8,128)(2,1)}), bf16[36,64,128]{2,0,1:T(8,128)(2,1)S(1)}, u32[]{:S(2)}, u32[]{:S(2)}) async-start(bf16[36,64,128]{2,0,1:T(8,128)(2,1)} %copy.44), calls=%async_computation.2 | async-start | bytes 1310720 | tf_op jit(solution)/shard_map/all_to_all | solution.py:168
  66.8 222.0 %reduce-scatter.3.cloned.1.call-start = ((), (), s32[]{:S(2)}) async-start(), calls=%async_computation.10 | async-start | bytes 1327104 | tf_op jit(solution)/shard_map/reduce_scatter | solution.py:174
  73.5 51.5 %copy-start.5 = (s32[8,8,36]{2,1,0:T(8,128)}, s32[8,8,36]{2,1,0:T(8,128)S(1)}, u32[]{:S(2)}) copy-start(s32[8,8,36]{2,1,0:T(8,128)S(1)} %copy.46) | copy-start | bytes 27652
  125.1 9.2 %copy-start.11 = (s32[3,768]{1,0:T(4,128)}, s32[3,768]{1,0:T(4,128)S(1)}, u32[]{:S(2)}) copy-start(s32[3,768]{1,0:T(4,128)S(1)} %get-tuple-element.680) | copy-start | bytes 27652 | tf_op jit(solution)/shard_map/while
  125.1 9.2 %copy-start.15 = (s32[2304]{0:T(1024)}, s32[2304]{0:T(1024)S(1)}, u32[]{:S(2)}) copy-start(s32[2304]{0:T(1024)S(1)} %get-tuple-element.694) | copy-start | bytes 27652 | tf_op jit(solution)/shard_map/while
  125.1 10.3 %copy-start.8 = (pred[3,768]{1,0:T(4,128)(4,1)}, pred[3,768]{1,0:T(4,128)(4,1)S(1)}, u32[]{:S(2)}) copy-start(pred[3,768]{1,0:T(4,128)(4,1)S(1)} %get-tuple-element.683) | copy-start | bytes 6916 | tf_op jit(solution)/shard_map/while
  140.2 5.2 %copy-start = (f32[1,768,2304]{2,1,0:T(8,128)S(1)}, f32[1,768,2304]{2,1,0:T(8,128)}, u32[]{:S(2)}) copy-start(f32[1,768,2304]{2,1,0:T(8,128)} %divide_multiply_fusion.3) | copy-start | bytes 21233668 | tf_op jit(solution)/shard_map/while
  147.6 3.0 copy-start.1
  147.6 10.2 %slice-start = ((s8[7077888]{0:T(1024)(128)(4,1)}), s8[2883584]{0:T(1024)(128)(4,1)S(1)}, s32[]{:S(2)}) async-start(s8[7077888]{0:T(1024)(128)(4,1)} %bitcast.194), calls=%async_computation.12 | async-start | bytes 5767168 | tf_op jit(solution)/shard_map/while
  153.5 4.3 %slice-start.1 = ((s8[7077888]{0:T(1024)(128)(4,1)}), s8[4194304]{0:T(1024)(128)(4,1)S(1)}, s32[]{:S(2)}) async-start(s8[7077888]{0:T(1024)(128)(4,1)} %bitcast.194), calls=%async_computation.13 | async-start | bytes 8388608 | tf_op jit(solution)/shard_map/while
  157.8 2.3 copy-start.9
  157.9 2.3 copy-start.12
  157.9 2.2 copy-start.16
  160.1 9.3 %copy-start.11 = (s32[3,768]{1,0:T(4,128)}, s32[3,768]{1,0:T(4,128)S(1)}, u32[]{:S(2)}) copy-start(s32[3,768]{1,0:T(4,128)S(1)} %get-tuple-element.680) | copy-start | bytes 27652 | tf_op jit(solution)/shard_map/while
  160.1 9.3 %copy-start.15 = (s32[2304]{0:T(1024)}, s32[2304]{0:T(1024)S(1)}, u32[]{:S(2)}) copy-start(s32[2304]{0:T(1024)S(1)} %get-tuple-element.694) | copy-start | bytes 27652 | tf_op jit(solution)/shard_map/while
  160.2 10.4 %copy-start.8 = (pred[3,768]{1,0:T(4,128)(4,1)}, pred[3,768]{1,0:T(4,128)(4,1)S(1)}, u32[]{:S(2)}) copy-start(pred[3,768]{1,0:T(4,128)(4,1)S(1)} %get-tuple-element.683) | copy-start | bytes 6916 | tf_op jit(solution)/shard_map/while
  175.3 5.2 %copy-start = (f32[1,768,2304]{2,1,0:T(8,128)S(1)}, f32[1,768,2304]{2,1,0:T(8,128)}, u32[]{:S(2)}) copy-start(f32[1,768,2304]{2,1,0:T(8,128)} %divide_multiply_fusion.3) | copy-start | bytes 21233668 | tf_op jit(solution)/shard_map/while
  182.7 3.0 copy-start.1
  182.7 10.6 %slice-start = ((s8[7077888]{0:T(1024)(128)(4,1)}), s8[2883584]{0:T(1024)(128)(4,1)S(1)}, s32[]{:S(2)}) async-start(s8[7077888]{0:T(1024)(128)(4,1)} %bitcast.194), calls=%async_computation.12 | async-start | bytes 5767168 | tf_op jit(solution)/shard_map/while
  188.6 4.7 %slice-start.1 = ((s8[7077888]{0:T(1024)(128)(4,1)}), s8[4194304]{0:T(1024)(128)(4,1)S(1)}, s32[]{:S(2)}) async-start(s8[7077888]{0:T(1024)(128)(4,1)} %bitcast.194), calls=%async_computation.13 | async-start | bytes 8388608 | tf_op jit(solution)/shard_map/while
  193.3 3.5 %copy-start.9 = (pred[3,768]{1,0:T(4,128)(4,1)S(1)}, pred[3,768]{1,0:T(4,128)(4,1)}, u32[]{:S(2)}) copy-start(pred[3,768]{1,0:T(4,128)(4,1)} %copy-done.8) | copy-start | bytes 6916 | tf_op jit(solution)/shard_map/while
  193.3 3.5 %copy-start.12 = (s32[3,768]{1,0:T(4,128)S(1)}, s32[3,768]{1,0:T(4,128)}, u32[]{:S(2)}) copy-start(s32[3,768]{1,0:T(4,128)} %copy-done.11) | copy-start | bytes 27652 | tf_op jit(solution)/shard_map/while
  193.3 3.5 %copy-start.16 = (s32[2304]{0:T(1024)S(1)}, s32[2304]{0:T(1024)}, u32[]{:S(2)}) copy-start(s32[2304]{0:T(1024)} %copy-done.15) | copy-start | bytes 27652 | tf_op jit(solution)/shard_map/while
  196.9 9.2 %copy-start.11 = (s32[3,768]{1,0:T(4,128)}, s32[3,768]{1,0:T(4,128)S(1)}, u32[]{:S(2)}) copy-start(s32[3,768]{1,0:T(4,128)S(1)} %get-tuple-element.680) | copy-start | bytes 27652 | tf_op jit(solution)/shard_map/while
  196.9 9.2 %copy-start.15 = (s32[2304]{0:T(1024)}, s32[2304]{0:T(1024)S(1)}, u32[]{:S(2)}) copy-start(s32[2304]{0:T(1024)S(1)} %get-tuple-element.694) | copy-start | bytes 27652 | tf_op jit(solution)/shard_map/while
  196.9 10.3 %copy-start.8 = (pred[3,768]{1,0:T(4,128)(4,1)}, pred[3,768]{1,0:T(4,128)(4,1)S(1)}, u32[]{:S(2)}) copy-start(pred[3,768]{1,0:T(4,128)(4,1)S(1)} %get-tuple-element.683) | copy-start | bytes 6916 | tf_op jit(solution)/shard_map/while
  212.0 5.2 %copy-start = (f32[1,768,2304]{2,1,0:T(8,128)S(1)}, f32[1,768,2304]{2,1,0:T(8,128)}, u32[]{:S(2)}) copy-start(f32[1,768,2304]{2,1,0:T(8,128)} %divide_multiply_fusion.3) | copy-start | bytes 21233668 | tf_op jit(solution)/shard_map/while
  219.4 3.0 copy-start.1
  219.4 10.6 %slice-start = ((s8[7077888]{0:T(1024)(128)(4,1)}), s8[2883584]{0:T(1024)(128)(4,1)S(1)}, s32[]{:S(2)}) async-start(s8[7077888]{0:T(1024)(128)(4,1)} %bitcast.194), calls=%async_computation.12 | async-start | bytes 5767168 | tf_op jit(solution)/shard_map/while
  225.3 4.7 %slice-start.1 = ((s8[7077888]{0:T(1024)(128)(4,1)}), s8[4194304]{0:T(1024)(128)(4,1)S(1)}, s32[]{:S(2)}) async-start(s8[7077888]{0:T(1024)(128)(4,1)} %bitcast.194), calls=%async_computation.13 | async-start | bytes 8388608 | tf_op jit(solution)/shard_map/while
  230.0 3.5 %copy-start.9 = (pred[3,768]{1,0:T(4,128)(4,1)S(1)}, pred[3,768]{1,0:T(4,128)(4,1)}, u32[]{:S(2)}) copy-start(pred[3,768]{1,0:T(4,128)(4,1)} %copy-done.8) | copy-start | bytes 6916 | tf_op jit(solution)/shard_map/while
  230.0 3.5 %copy-start.12 = (s32[3,768]{1,0:T(4,128)S(1)}, s32[3,768]{1,0:T(4,128)}, u32[]{:S(2)}) copy-start(s32[3,768]{1,0:T(4,128)} %copy-done.11) | copy-start | bytes 27652 | tf_op jit(solution)/shard_map/while
  230.0 3.5 %copy-start.16 = (s32[2304]{0:T(1024)S(1)}, s32[2304]{0:T(1024)}, u32[]{:S(2)}) copy-start(s32[2304]{0:T(1024)} %copy-done.15) | copy-start | bytes 27652 | tf_op jit(solution)/shard_map/while
  233.6 22.6 %copy-start.4 = (bf16[3,768,1,128]{3,1,0,2:T(8,128)(2,1)S(1)}, bf16[3,768,1,128]{3,1,0,2:T(8,128)(2,1)}, u32[]{:S(2)}) copy-start(bf16[3,768,1,128]{3,1,0,2:T(8,128)(2,1)} %get-tuple-element.181) | copy-start | bytes 1769476
  235.6 46.9 %all-to-all-start.4 = ((bf16[64,36,128]{2,1,0:T(8,128)(2,1)}), bf16[64,36,128]{2,1,0:T(8,128)(2,1)S(1)}, u32[]{:S(2)}, u32[]{:S(2)}) async-start(bf16[64,36,128]{2,1,0:T(8,128)(2,1)} %all_to_all.112), calls=%async_computation.4 | async-start | bytes 1310720 | tf_op jit(solution)/shard_map/all_to_all | solution.py:193
  255.4 72.2 %reduce-scatter.5.cloned.1.call-start = ((), (), s32[]{:S(2)}) async-start(), calls=%async_computation.11 | async-start | bytes 1327104 | tf_op jit(solution)/shard_map/reduce_scatter | solution.py:175
  282.5 26.2 %all-to-all-start.5 = ((bf16[64,36,128]{2,1,0:T(8,128)(2,1)}), bf16[64,36,128]{2,1,0:T(8,128)(2,1)S(1)}, u32[]{:S(2)}, u32[]{:S(2)}) async-start(bf16[64,36,128]{2,1,0:T(8,128)(2,1)} %all_to_all.116), calls=%async_computation.5 | async-start | bytes 1310720 | tf_op jit(solution)/shard_map/all_to_all | solution.py:194
  308.7 20.5 %all-to-all-start.6 = ((bf16[8,36,128]{2,1,0:T(8,128)(2,1)}), bf16[8,36,128]{2,1,0:T(8,128)(2,1)S(1)}, u32[]{:S(2)}, u32[]{:S(2)}) async-start(bf16[8,36,128]{2,1,0:T(8,128)(2,1)} %all_to_all.120), calls=%async_computation.7 | async-start | bytes 163840 | tf_op jit(solution)/shard_map/all_to_all | solution.py:178
  329.2 14.0 %all-to-all-start.7 = ((bf16[8,36,128]{2,1,0:T(8,128)(2,1)}), bf16[8,36,128]{2,1,0:T(8,128)(2,1)S(1)}, u32[]{:S(2)}, u32[]{:S(2)}) async-start(bf16[8,36,128]{2,1,0:T(8,128)(2,1)} %all_to_all.122), calls=%async_computation.9 | async-start | bytes 163840 | tf_op jit(solution)/shard_map/all_to_all | solution.py:181
  (1 other events, 1.4 us)
Sparse Core Ops, SparseCore 0:
  233.7 54.7 reduce-scatter.2
  291.0 36.5 reduce-scatter.4
where the time goes:
time: 352 us; the launch traced here: 351 us
  waiting for transfers between devices  83 us (24%)
  starting transfers between devices  67.7 us (19%)
  matrix products  63.5 us (18%)
  blocking collectives  49.5 us (14%)
  other arithmetic  46.8 us (13%)
  local copies, waits for them, and re-layouts  25 us (7%)
  between operations  14.5 us (4%)
    all_gather x1, blocking collectives, shards(): lax.all_gather(key_split, 'head', axis=0, tiled=True)  27.3 us
    all_to_all x1, waiting for transfers between devices, shards(): lax.all_to_all(out_heads, ('seq', 'head'), split_axis=0, concat_axis=1, t...  25.4 us
    gather x4, other arithmetic, shards(): jnp.repeat(counts, capacity, total_repeat_length=routed_count)  23 us
    all_gather x1, blocking collectives, shards(): lax.all_gather(value_split, 'head', axis=0, tiled=True)  22.2 us
    all_to_all x1, starting transfers between devices, shards(): lax.all_to_all(out_heads, ('seq', 'head'), split_axis=0, concat_axis=1, t...  19.8 us
    all_to_all x1, waiting for transfers between devices, shards(): lax.all_to_all(query_rotated, ('seq', 'head'), split_axis=1, concat_axis=...  18.3 us
    all_to_all x1, waiting for transfers between devices, shards(): lax.all_to_all(grad_heads, ('seq', 'head'), split_axis=0, concat_axis=1,...  18.2 us
    dot_general x3, matrix products, block_step(): jnp.einsum('hbk,kd->bhd', probs_low, value_block, preferred_element_type=...  15.6 us
  transfers between devices with their start and end apart: 10, of which 7 were waited for; matrix products, arithmetic and copies ran while one was open for 5% of the time, Pallas kernels for 0%

commit v1 on v0

v1 whole, which is shorter than its diff:
```python
import functools

import jax
import jax.numpy as jnp
import numpy as np
from jax import lax
from jax.experimental import pallas as pl
from jax.experimental.pallas import tpu as pltpu
from jax.sharding import PartitionSpec as P

QUERY_HEADS = 64
GROUPS = 8
HEADS = 8
WIDTH = 128
NSEQ = 8
NZ = 8
ROWS = 36
CAP = 288
SLOTS = 2304
CHUNK = 384
ROPE_BASE = 500000.0
BIG = 1 << 20
SCALE = 1.0 / np.sqrt(128.0)
SCALE2 = float(SCALE * np.log2(np.e))
MESH = pl.DeviceIdType.MESH
F32 = jnp.float32
BF16 = jnp.bfloat16


def dot_nt(a, b):
    return lax.dot_general(a, b, (((1,), (1,)), ((), ())), preferred_element_type=F32)


def dot_tn(a, b):
    return lax.dot_general(a, b, (((0,), (0,)), ((), ())), preferred_element_type=F32)


def dot_nn(a, b):
    return jnp.dot(a, b, preferred_element_type=F32)


def roll_half(x):
    return pltpu.roll(x, WIDTH // 2, 1)


def rope(x, cos, sin):
    return x * cos + roll_half(x) * sin


def rope_t(x, cos, sin):
    return x * cos - roll_half(x) * sin


HOPS = ((4, 3), (3, 4))


def kernel(
    counts, cos, sin, q_in, k_in, v_in, g_in,
    att_out, dq_out, dk_out, dv_out,
    q_got, g_got, kv_got, kv_ring, stage, q_all, g_all, k_all, v_all, kv_stage,
    slot, limit, s_scr, dk_acc, dv_acc, o_send, dq_send, part, rs_out, rs_in, kv_send,
    sem_kv_s, sem_kv_r, sem_q_s, sem_q_r, sem_g_s, sem_g_r, sem_ag_s, sem_ag_r,
    sem_o_s, sem_o_r, sem_dq_s, sem_dq_r, sem_rs_s, sem_rs_r, sem_b_s, sem_b_r,
):
    me = lax.axis_index("seq")
    mz = lax.axis_index("head")
    right = lax.rem(mz + 1, NZ)
    left = lax.rem(mz + NZ - 1, NZ)
    nbr = (right, left)

    barrier = pltpu.get_barrier_semaphore()
    for d in range(1, NSEQ):
        pl.semaphore_signal(barrier, inc=1, device_id={"seq": lax.rem(me + d, NSEQ)}, device_id_type=MESH)
    for z in nbr:
        pl.semaphore_signal(barrier, inc=1, device_id={"head": z}, device_id_type=MESH)
    pl.semaphore_wait(barrier, NSEQ - 1 + 2)

    def remote(src, dst, ss, rs, **where):
        return pltpu.make_async_remote_copy(
            src_ref=src, dst_ref=dst, send_sem=ss, recv_sem=rs, device_id=where, device_id_type=MESH
        )

    kv_in = (k_in, v_in)

    def kv_copy(i, src, to):
        return remote(
            kv_in[i].at[:, pl.ds(pl.multiple_of(to * WIDTH, WIDTH), WIDTH)],
            kv_got.at[i, src], sem_kv_s.at[i, to], sem_kv_r.at[i, src], seq=to,
        )

    def wide_copy(arr, got, ss, rs, src, to):
        return remote(
            arr.at[:, pl.ds(pl.multiple_of(to * 1024, 1024), 1024)],
            got.at[src], ss.at[to], rs.at[src], seq=to,
        )

    q_copy = functools.partial(wide_copy, q_in, q_got, sem_q_s, sem_q_r)
    g_copy = functools.partial(wide_copy, g_in, g_got, sem_g_s, sem_g_r)
    others = [lax.rem(me + d, NSEQ) for d in range(1, NSEQ)]
    own_kv = [
        pltpu.make_async_copy(
            kv_in[i].at[:, pl.ds(pl.multiple_of(me * WIDTH, WIDTH), WIDTH)], kv_got.at[i, me], sem_kv_r.at[i, me]
        )
        for i in range(2)
    ]
    own_q = pltpu.make_async_copy(
        q_in.at[:, pl.ds(pl.multiple_of(me * 1024, 1024), 1024)], q_got.at[me], sem_q_r.at[me]
    )
    own_g = pltpu.make_async_copy(
        g_in.at[:, pl.ds(pl.multiple_of(me * 1024, 1024), 1024)], g_got.at[me], sem_g_r.at[me]
    )
    for to in others:
        for i in range(2):
            kv_copy(i, me, to).start()
    for c in own_kv:
        c.start()
    own_q.start()
    own_g.start()
    for to in others:
        q_copy(me, to).start()
    for to in others:
        g_copy(me, to).start()

    row_in = lax.broadcasted_iota(jnp.int32, (ROWS, WIDTH), 0) + mz * ROWS
    for h in range(HEADS):
        limit[h * ROWS : (h + 1) * ROWS, :] = row_in
    lane = lax.broadcasted_iota(jnp.int32, (8, SLOTS), 1)
    keep = lane
    for s in range(NSEQ):
        dead = (lane >= s * CAP + counts[s]) & (lane < (s + 1) * CAP)
        keep = jnp.where(dead, BIG, keep)
    slot[...] = keep

    for c in own_kv:
        c.wait()
    for src in others:
        for i in range(2):
            kv_copy(i, src, src).wait_recv()
    for s in range(NSEQ):
        x = rope(kv_got[0, s].astype(F32), cos[s], sin[s])
        kv_stage[0, s * ROWS : (s + 1) * ROWS, :] = x
        kv_stage[1, s * ROWS : (s + 1) * ROWS, :] = kv_got[1, s].astype(F32)
    for i in range(2):
        kv_ring[i, mz] = kv_stage[i].astype(BF16)

    def ag_copy(i, dr, t, z):
        return remote(
            kv_ring.at[i, z], kv_ring.at[i, z], sem_ag_s.at[i, dr, t], sem_ag_r.at[i, dr, t], head=nbr[dr]
        )

    for i in range(2):
        for dr in range(2):
            ag_copy(i, dr, 0, mz).start()

    def place_rows(s):
        for h in range(HEADS):
            cols = slice(h * WIDTH, (h + 1) * WIDTH)
            x = rope(q_got[s, :, cols].astype(F32), cos[s], sin[s])
            stage[0, h * ROWS : (h + 1) * ROWS, :] = x
            stage[1, h * ROWS : (h + 1) * ROWS, :] = g_got[s, :, cols].astype(F32)
        q_all[s] = stage[0].astype(BF16)
        g_all[s] = stage[1].astype(BF16)

    for t in range(4):
        for i in range(2):
            for dr in range(2):
                n = HOPS[i][dr]
                if t < n:
                    step = -(t + 1) if dr == 0 else t + 1
                    z = lax.rem(mz + step + NZ, NZ)
                    ag_copy(i, dr, t, z).wait_recv()
                    if t + 1 < n:
                        ag_copy(i, dr, t + 1, z).start()

    own_q.wait()
    own_g.wait()
    for src in others:
        q_copy(src, src).wait_recv()
        g_copy(src, src).wait_recv()

    def place_step(s, carry):
        place_rows(s)
        return carry

    lax.fori_loop(0, NSEQ, place_step, 0)

    for i, whole in ((0, k_all), (1, v_all)):
        for z in range(NZ):
            x = kv_ring[i, z].astype(F32)
            for s in range(NSEQ):
                part[0, s * CAP + z * ROWS : s * CAP + (z + 1) * ROWS, :] = x[s * ROWS : (s + 1) * ROWS]
        whole[...] = part[0].astype(BF16)

    dk_acc[...] = jnp.zeros_like(dk_acc)
    dv_acc[...] = jnp.zeros_like(dv_acc)

    def out_copy(send, out, ss, rs, src, to):
        return remote(
            send.at[to], out.at[:, pl.ds(pl.multiple_of(src * 1024, 1024), 1024)], ss.at[to], rs.at[src], seq=to
        )

    o_copy = functools.partial(out_copy, o_send, att_out, sem_o_s, sem_o_r)
    dq_copy = functools.partial(out_copy, dq_send, dq_out, sem_dq_s, sem_dq_r)

    def own_out(send, out, rs):
        return pltpu.make_async_copy(
            send.at[me], out.at[:, pl.ds(pl.multiple_of(me * 1024, 1024), 1024)], rs.at[me]
        )

    lanes = CHUNK // WIDTH
    for s in reversed(range(NSEQ)):
        n = ((s + 1) * CAP + CHUNK - 1) // CHUNK
        qb = q_all[s]
        gb = g_all[s]
        lim = limit[...] + s * CAP
        live = (limit[...] < counts[s]).astype(F32)
        top = jnp.full((CAP, WIDTH), -1e30, F32)
        for c in range(n):
            cols = slice(c * CHUNK, (c + 1) * CHUNK)
            sc = dot_nt(qb, k_all[cols, :])
            for t in range(lanes):
                lo = c * CHUNK + t * WIDTH
                x = jnp.where(slot[0:1, lo : lo + WIDTH] <= lim, sc[:, t * WIDTH : (t + 1) * WIDTH], -1e30)
                top = jnp.maximum(top, x)
                s_scr[:, lo : lo + WIDTH] = x
        top = jnp.broadcast_to(jnp.max(top, 1, keepdims=True), (CAP, WIDTH))
        acc = jnp.zeros((CAP, WIDTH), F32)
        total = jnp.zeros((CAP, WIDTH), F32)
        for c in range(n):
            cols = slice(c * CHUNK, (c + 1) * CHUNK)
            ws = []
            for t in range(lanes):
                lo = c * CHUNK + t * WIDTH
                w = jnp.exp2((s_scr[:, lo : lo + WIDTH] - top) * SCALE2)
                s_scr[:, lo : lo + WIDTH] = w
                total = total + w
                ws.append(w.astype(BF16))
            acc = acc + dot_nn(jnp.concatenate(ws, 1), v_all[cols, :])
        inv = live / jnp.sum(total, 1, keepdims=True)
        att = (acc * inv).astype(BF16).astype(F32)
        delta = jnp.sum(gb.astype(F32) * att, 1, keepdims=True)
        delta = jnp.broadcast_to(delta, (CAP, WIDTH))
        for h in range(HEADS):
            o_send[s, :, h * WIDTH : (h + 1) * WIDTH] = att[h * ROWS : (h + 1) * ROWS].astype(BF16)

        @pl.when(me == s)
        def _():
            own_out(o_send, att_out, sem_o_r).start()

        @pl.when(me != s)
        def _():
            o_copy(me, s).start()

        dq = jnp.zeros((CAP, WIDTH), F32)
        for c in range(n):
            cols = slice(c * CHUNK, (c + 1) * CHUNK)
            dp = dot_nt(gb, v_all[cols, :])
            ps, ds = [], []
            for t in range(lanes):
                lo = c * CHUNK + t * WIDTH
                p = s_scr[:, lo : lo + WIDTH] * inv
                ps.append(p.astype(BF16))
                ds.append((p * (dp[:, t * WIDTH : (t + 1) * WIDTH] - delta)).astype(BF16))
            p = jnp.concatenate(ps, 1)
            d = jnp.concatenate(ds, 1)
            dv_acc[cols, :] += dot_tn(p, gb)
            dk_acc[cols, :] += dot_tn(d, qb)
            dq = dq + dot_nn(d, k_all[cols, :])
        dq = dq * SCALE
        for h in range(HEADS):
            x = rope_t(dq[h * ROWS : (h + 1) * ROWS], cos[s], sin[s])
            dq_send[s, :, h * WIDTH : (h + 1) * WIDTH] = x.astype(BF16)

        @pl.when(me == s)
        def _():
            own_out(dq_send, dq_out, sem_dq_r).start()

        @pl.when(me != s)
        def _():
            dq_copy(me, s).start()

    for i, acc in ((0, dk_acc), (1, dv_acc)):
        for z in range(NZ):
            for s in range(NSEQ):
                lo = s * CAP + z * ROWS
                part[i, z * CAP + s * ROWS : z * CAP + (s + 1) * ROWS, :] = acc[lo : lo + ROWS, :]

    def mine(i, z):
        return part[i, pl.ds(pl.multiple_of(z * CAP, CAP), CAP), :]

    def rs_copy(i, dr, t):
        return remote(
            rs_out.at[i, dr, t], rs_in.at[i, dr, t], sem_rs_s.at[i, dr, t], sem_rs_r.at[i, dr, t], head=nbr[dr]
        )

    for t in range(4):
        for i in range(2):
            for dr in range(2):
                n = HOPS[i][dr]
                if t < n:
                    step = n - t if dr == 0 else t - n
                    z = lax.rem(mz + step + NZ, NZ)
                    x = mine(i, z)
                    if t > 0:
                        rs_copy(i, dr, t - 1).wait_recv()
                        x = x + rs_in[i, dr, t - 1].astype(F32)
                    rs_out[i, dr, t] = x.astype(BF16)
                    rs_copy(i, dr, t).start()

    kv_out = (dk_out, dv_out)

    def back_copy(i, src, to):
        return remote(
            kv_send.at[i, to],
            kv_out[i].at[:, pl.ds(pl.multiple_of(src * WIDTH, WIDTH), WIDTH)],
            sem_b_s.at[i, to], sem_b_r.at[i, src], seq=to,
        )

    own_back = [
        pltpu.make_async_copy(
            kv_send.at[i, me],
            kv_out[i].at[:, pl.ds(pl.multiple_of(me * WIDTH, WIDTH), WIDTH)],
            sem_b_r.at[i, me],
        )
        for i in range(2)
    ]
    for i in range(2):
        x = mine(i, mz)
        for dr in range(2):
            n = HOPS[i][dr]
            rs_copy(i, dr, n - 1).wait_recv()
            x = x + rs_in[i, dr, n - 1].astype(F32)
        for s in range(NSEQ):
            y = x[s * ROWS : (s + 1) * ROWS]
            if i == 0:
                y = rope_t(y * SCALE, cos[s], sin[s])
            kv_send[i, s] = y.astype(BF16)
        own_back[i].start()
        for to in others:
            back_copy(i, me, to).start()

    own_out(o_send, att_out, sem_o_r).wait()
    own_out(dq_send, dq_out, sem_dq_r).wait()
    for c in own_back:
        c.wait()
    for src in others:
        o_copy(src, me).wait_recv()
        dq_copy(src, me).wait_recv()
        for i in range(2):
            back_copy(i, src, me).wait_recv()
    for to in others:
        for i in range(2):
            kv_copy(i, me, to).wait_send()
            back_copy(i, me, to).wait_send()
        q_copy(me, to).wait_send()
        g_copy(me, to).wait_send()
        o_copy(me, to).wait_send()
        dq_copy(me, to).wait_send()
    for i in range(2):
        for dr in range(2):
            for t in range(HOPS[i][dr]):
                ag_copy(i, dr, t, mz).wait_send()
                rs_copy(i, dr, t).wait_send()


def shards(queries, routed_keys, routed_values, output_gradient, positions, counts):
    mz = lax.axis_index("head")
    local_pos = lax.dynamic_slice(positions.reshape(NSEQ, CAP), (0, mz * ROWS), (NSEQ, ROWS))
    inverse_freq = jnp.float32(ROPE_BASE) ** (-(jnp.arange(WIDTH // 2, dtype=F32) * 2.0 / WIDTH))
    angle = local_pos.astype(F32)[:, :, None] * inverse_freq
    c, s = jnp.cos(angle), jnp.sin(angle)
    cos = jnp.concatenate([c, c], -1)
    sin = jnp.concatenate([-s, s], -1)
    anywhere = pl.BlockSpec(memory_space=pl.ANY)
    vmem = pl.BlockSpec(memory_space=pltpu.VMEM)
    smem = pl.BlockSpec(memory_space=pltpu.SMEM)
    dma = pltpu.SemaphoreType.DMA
    out = jax.ShapeDtypeStruct
    return pl.pallas_call(
        kernel,
        out_shape=[
            out((ROWS, QUERY_HEADS * WIDTH), BF16),
            out((ROWS, QUERY_HEADS * WIDTH), BF16),
            out((ROWS, GROUPS * WIDTH), BF16),
            out((ROWS, GROUPS * WIDTH), BF16),
        ],
        in_specs=[smem, vmem, vmem, anywhere, anywhere, anywhere, anywhere],
        out_specs=[anywhere] * 4,
        scratch_shapes=[
            pltpu.VMEM((NSEQ, ROWS, HEADS * WIDTH), BF16),
            pltpu.VMEM((NSEQ, ROWS, HEADS * WIDTH), BF16),
            pltpu.VMEM((2, NSEQ, ROWS, WIDTH), BF16),
            pltpu.VMEM((2, NZ, CAP, WIDTH), BF16),
            pltpu.VMEM((2, CAP, WIDTH), F32),
            pltpu.VMEM((NSEQ, CAP, WIDTH), BF16),
            pltpu.VMEM((NSEQ, CAP, WIDTH), BF16),
            pltpu.VMEM((SLOTS, WIDTH), BF16),
            pltpu.VMEM((SLOTS, WIDTH), BF16),
            pltpu.VMEM((2, CAP, WIDTH), F32),
            pltpu.VMEM((8, SLOTS), jnp.int32),
            pltpu.VMEM((CAP, WIDTH), jnp.int32),
            pltpu.VMEM((CAP, SLOTS), F32),
            pltpu.VMEM((SLOTS, WIDTH), F32),
            pltpu.VMEM((SLOTS, WIDTH), F32),
            pltpu.VMEM((NSEQ, ROWS, HEADS * WIDTH), BF16),
            pltpu.VMEM((NSEQ, ROWS, HEADS * WIDTH), BF16),
            pltpu.VMEM((2, SLOTS, WIDTH), F32),
            pltpu.VMEM((2, 2, 4, CAP, WIDTH), BF16),
            pltpu.VMEM((2, 2, 4, CAP, WIDTH), BF16),
            pltpu.VMEM((2, NSEQ, ROWS, WIDTH), BF16),
            dma((2, NSEQ)), dma((2, NSEQ)), dma((NSEQ,)), dma((NSEQ,)), dma((NSEQ,)), dma((NSEQ,)),
            dma((2, 2, 4)), dma((2, 2, 4)),
            dma((NSEQ,)), dma((NSEQ,)), dma((NSEQ,)), dma((NSEQ,)),
            dma((2, 2, 4)), dma((2, 2, 4)), dma((2, NSEQ)), dma((2, NSEQ)),
        ],
        compiler_params=pltpu.CompilerParams(
            collective_id=0, has_side_effects=True, vmem_limit_bytes=48 * 2**20
        ),
        cost_estimate=pl.CostEstimate(flops=5 * 10**9, bytes_accessed=4 * 10**6, transcendentals=3 * 10**6),
    )(counts, cos, sin, queries, routed_keys, routed_values, output_gradient)


def solution(mesh):
    rows = P(("dp", "seq", "head"), None)
    return jax.shard_map(
        shards, mesh=mesh, in_specs=(rows, rows, rows, rows, P("dp"), P("dp")), out_specs=(rows,) * 4, check_vma=False
    )
```

time: 352 us -> 84.9 us (0.24)
  waiting for transfers between devices: 83 us -> 0 us
  Pallas kernels: 0 us -> 76.9 us
  starting transfers between devices: 67.7 us -> 0 us
  matrix products: 63.5 us -> 0 us
  blocking collectives: 49.5 us -> 0 us
  other arithmetic: 46.8 us -> 0.89 us
  local copies, waits for them, and re-layouts: 25 us -> 6.22 us
  between operations: 14.5 us -> 0.68 us
    pallas_call x0 -> x1, Pallas kernels: none -> 76.9 us  [shards(): pl.pallas_call(kernel, out_shape=[out((ROWS, QUERY_HEADS * WIDTH), BF16),...]
    all_to_all x8 -> x0, waiting for transfers between devices: 71.7 us -> none  [the longest x1 25.4 us: shards(): lax.all_to_all(out_heads, ('seq', 'head'), split_axis=0, concat_axis=1, t...]
    all_to_all x8 -> x0, starting transfers between devices: 67.7 us -> none  [the longest x1 19.8 us: shards(): lax.all_to_all(out_heads, ('seq', 'head'), split_axis=0, concat_axis=1, t...]
    dot_general x18 -> x0, matrix products: 63.5 us -> none  [the longest x3 15.6 us: block_step(): jnp.einsum('hbk,kd->bhd', probs_low, value_block, preferred_element_type=...]
    all_gather x2 -> x0, blocking collectives: 49.5 us -> none  [the longest x1 27.3 us: shards(): lax.all_gather(key_split, 'head', axis=0, tiled=True)]
    gather x4 -> x0, other arithmetic: 23 us -> none  [shards(): jnp.repeat(counts, capacity, total_repeat_length=routed_count)]
    mul x3 -> x0, other arithmetic: 10.9 us -> none  [block_step(): probs = weights / row_total * live_part.astype(jnp.float32)[None, :, None]]
    reduce_scatter x2 -> x0, waiting for transfers between devices: 10.5 us -> none  [the longest x1 10.5 us: shards(): lax.psum_scatter(value_grad, 'head', scatter_dimension=0, tiled=True)]
  transfers between devices with their start and end apart: 10 -> 0, of which waited for: 7 -> 0; matrix products, arithmetic and copies ran while one was open for 5% -> 0% of each run, Pallas kernels for 0% -> 0%
where the time goes in v1:
time: 84.9 us; the launch traced here: 84.7 us
  Pallas kernels  76.9 us (91%)
  local copies, waits for them, and re-layouts  6.22 us (7%)
  other arithmetic  0.89 us (1%)
    pallas_call x1, Pallas kernels, shards(): pl.pallas_call(kernel, out_shape=[out((ROWS, QUERY_HEADS * WIDTH), BF16),...  76.9 us
    unnamed x16, local copies, waits for them, and re-layouts  6.15 us

profile of v1, /device:TPU:1, one launch (start us, length us, event | category | flops | bytes accessed | tf_op | source)
XLA Modules:
  0.0 84.7 jit_solution(11840984053322696438)
XLA Ops:
  0.6 0.0 copy-start.5
  0.7 0.7 copy-done.5
  1.3 0.1 reshape.18
  1.4 0.1 dynamic-slice_convert_fusion
  1.5 0.0 copy-start
  1.5 0.0 copy-start.1
  1.5 0.6 fusion
  2.1 0.2 pad_maximum_fusion
  2.3 0.0 copy-start.4
  2.3 0.3 copy-done
  2.6 0.2 copy-done.1
  2.8 0.3 copy-done.4
  3.1 0.0 copy-start.2
  3.1 0.9 %copy-done.2 = bf16[36,1024]{1,0:T(8,128)(2,1)S(1)} copy-done((bf16[36,1024]{1,0:T(8,128)(2,1)S(1)}, bf16[36,1024]{1,0:T(8,128)(2,1)}, u32[]{:S(2)}) %copy-start.2) | copy-done | bytes 73752
  4.0 0.0 copy-start.3
  4.0 0.9 %copy-done.3 = bf16[36,1024]{1,0:T(8,128)(2,1)S(1)} copy-done((bf16[36,1024]{1,0:T(8,128)(2,1)S(1)}, bf16[36,1024]{1,0:T(8,128)(2,1)}, u32[]{:S(2)}) %copy-start.3) | copy-done | bytes 73752
  4.8 76.9 %shard_map.93 = (bf16[36,8192]{1,0:T(8,128)(2,1)S(1)}, bf16[36,8192]{1,0:T(8,128)(2,1)S(1)}, bf16[36,1024]{1,0:T(8,128)(2,1)S(1)}, bf16[36,1024]{1,0:T(8,128)(2,1)S(1)}) custom-call(s32[8]{0:T(128)S(1)} %copy-done.4, f32[8,36,128]{2,1,0:T(8,128)S(1)} %get-tuple-element.7.cos, f32[8,36,128]{2,1,0:T(8,128)S(1)} %get-tuple-element.8.sin, ...), custom_call_target="tpu_custom_call" | custom-call | flops 5000000000 | bytes 4000000 | tf_op jit(solution)/shard_map/pallas_call | solution.py:379
  81.8 0.8 copy.14
  82.6 0.8 copy.15
  83.4 0.6 copy.16
  84.1 0.6 copy.17
  (1 shorter events, 0.0 us)
Async XLA Ops:
  0.6 0.7 copy-start.5
  1.5 1.1 %copy-start = (bf16[36,8192]{1,0:T(8,128)(2,1)S(1)}, bf16[36,8192]{1,0:T(8,128)(2,1)}, u32[]{:S(2)}) copy-start(bf16[36,8192]{1,0:T(8,128)(2,1)} %q_in.1) | copy-start | bytes 1769476
  1.5 1.3 %copy-start.1 = (bf16[36,8192]{1,0:T(8,128)(2,1)S(1)}, bf16[36,8192]{1,0:T(8,128)(2,1)}, u32[]{:S(2)}) copy-start(bf16[36,8192]{1,0:T(8,128)(2,1)} %g_in.1) | copy-start | bytes 1769476
  2.3 0.8 copy-start.4
  3.1 0.9 %copy-start.2 = (bf16[36,1024]{1,0:T(8,128)(2,1)S(1)}, bf16[36,1024]{1,0:T(8,128)(2,1)}, u32[]{:S(2)}) copy-start(bf16[36,1024]{1,0:T(8,128)(2,1)} %k_in.1) | copy-start | bytes 221188
  4.0 0.9 %copy-start.3 = (bf16[36,1024]{1,0:T(8,128)(2,1)S(1)}, bf16[36,1024]{1,0:T(8,128)(2,1)}, u32[]{:S(2)}) copy-start(bf16[36,1024]{1,0:T(8,128)(2,1)} %v_in.1) | copy-start | bytes 221188

commit v2 on v1

v2 whole, which is shorter than its diff:
```python
import functools

import jax
import jax.numpy as jnp
import numpy as np
from jax import lax
from jax.experimental import pallas as pl
from jax.experimental.pallas import tpu as pltpu
from jax.sharding import PartitionSpec as P

QUERY_HEADS = 64
GROUPS = 8
HEADS = 8
WIDTH = 128
NSEQ = 8
NZ = 8
ROWS = 36
CAP = 288
SLOTS = 2304
PAIR = 2 * ROWS
WIDEST = 640
ROPE_BASE = 500000.0
BIG = 1 << 20
SCALE = 1.0 / np.sqrt(128.0)
SCALE2 = float(SCALE * np.log2(np.e))
MESH = pl.DeviceIdType.MESH
F32 = jnp.float32
BF16 = jnp.bfloat16


def dot_nt(a, b):
    return lax.dot_general(a, b, (((1,), (1,)), ((), ())), preferred_element_type=F32)


def dot_tn(a, b):
    return lax.dot_general(a, b, (((0,), (0,)), ((), ())), preferred_element_type=F32)


def dot_nn(a, b):
    return jnp.dot(a, b, preferred_element_type=F32)


def roll_half(x):
    return pltpu.roll(x, WIDTH // 2, 1)


def rope(x, cos, sin):
    return x * cos + roll_half(x) * sin


def rope_t(x, cos, sin):
    return x * cos - roll_half(x) * sin


OFFSETS = ((0, -1), (1, -2), (2, -3), (3, 4))
PLACE = {o: (q, w) for q, pair in enumerate(OFFSETS) for w, o in enumerate(pair)}
WIDE = tuple(-(-PAIR * (s + 1) // WIDTH) * WIDTH for s in range(NSEQ))
START = tuple(sum(WIDE[:s]) for s in range(NSEQ))
STORE = sum(WIDE)
FAR, THIRD, SECOND, FIRST = range(4)
DISTANCE = (4, 3, 2, 1)


def kernel(
    pos_in, counts_in, q_in, k_in, v_in, g_in,
    att_out, dq_out, dk_out, dv_out,
    pos, counts, pos_row, cos, sin, q_own, g_own, k_own, v_own,
    q_got, g_got, kv_got, kv_ring, stage, q_all, g_all, pair_stage, k_all, v_all,
    slot, limit, w_all, ds_all, top_all, sum_all, acc_all, inv_all, delta_all, att_all,
    dk_acc, dv_acc, o_send, dq_send, rs_out, rs_in, kv_send,
    sem_p, sem_in, sem_kv_s, sem_kv_r, sem_q_s, sem_q_r, sem_g_s, sem_g_r, sem_ag_s, sem_ag_r,
    sem_o_s, sem_o_r, sem_dq_s, sem_dq_r, sem_rs_s, sem_rs_r, sem_b_s, sem_b_r,
):
    me = lax.axis_index("seq")
    mz = lax.axis_index("head")

    def away(o):
        return lax.rem(mz + (o + NZ), NZ)

    barrier = pltpu.get_barrier_semaphore()
    for d in range(1, NSEQ):
        pl.semaphore_signal(barrier, inc=1, device_id={"seq": lax.rem(me + d, NSEQ)}, device_id_type=MESH)
    for o in (1, -1, 2, -2):
        pl.semaphore_signal(barrier, inc=1, device_id={"head": away(o)}, device_id_type=MESH)
    get_pos = pltpu.make_async_copy(pos_in, pos, sem_p.at[0])
    get_counts = pltpu.make_async_copy(counts_in, counts, sem_p.at[1])
    loads = [
        pltpu.make_async_copy(src, dst, sem_in.at[i])
        for i, (src, dst) in enumerate(((k_in, k_own), (v_in, v_own), (q_in, q_own), (g_in, g_own)))
    ]
    for c in loads:
        c.start()
    get_pos.start()
    get_counts.start()

    def remote(src, dst, ss, rs, **where):
        return pltpu.make_async_remote_copy(
            src_ref=src, dst_ref=dst, send_sem=ss, recv_sem=rs, device_id=where, device_id_type=MESH
        )

    def columns(i, width):
        return pl.ds(pl.multiple_of(i * width, width), width)

    kv_in = (k_own, v_own)

    def kv_copy(i, src, to):
        return remote(
            kv_in[i].at[:, columns(to, WIDTH)], kv_got.at[i, src], sem_kv_s.at[i, to], sem_kv_r.at[i, src], seq=to
        )

    def wide_copy(arr, got, ss, rs, src, to):
        return remote(arr.at[:, columns(to, 1024)], got.at[src], ss.at[to], rs.at[src], seq=to)

    q_copy = functools.partial(wide_copy, q_own, q_got, sem_q_s, sem_q_r)
    g_copy = functools.partial(wide_copy, g_own, g_got, sem_g_s, sem_g_r)
    others = [lax.rem(me + d, NSEQ) for d in range(1, NSEQ)]
    own_kv = [
        pltpu.make_async_copy(kv_in[i].at[:, columns(me, WIDTH)], kv_got.at[i, me], sem_kv_r.at[i, me])
        for i in range(2)
    ]
    own_q = pltpu.make_async_copy(q_own.at[:, columns(me, 1024)], q_got.at[me], sem_q_r.at[me])
    own_g = pltpu.make_async_copy(g_own.at[:, columns(me, 1024)], g_got.at[me], sem_g_r.at[me])
    pl.semaphore_wait(barrier, NSEQ - 1 + 4)
    loads[0].wait()
    loads[1].wait()
    for to in others:
        for i in range(2):
            kv_copy(i, me, to).start()
    for c in own_kv:
        c.start()
    loads[2].wait()
    for to in others:
        q_copy(me, to).start()
    own_q.start()
    loads[3].wait()
    for to in others:
        g_copy(me, to).start()
    own_g.start()

    get_pos.wait()
    get_counts.wait()
    for s in range(NSEQ):
        for r in range(ROWS):
            at = pos[s * CAP + mz * ROWS + r].astype(F32)
            pos_row[s, r : r + 1, :] = jnp.full((1, WIDTH), at, F32)
    lane = lax.broadcasted_iota(jnp.int32, (1, WIDTH), 1)
    upper = lane >= WIDTH // 2
    half = jnp.where(upper, lane - WIDTH // 2, lane).astype(F32)
    freq = jnp.float32(ROPE_BASE) ** (-(half * 2.0 / WIDTH))
    for s in range(NSEQ):
        angle = pos_row[s] * freq
        cos[s] = jnp.cos(angle)
        sine = jnp.sin(angle)
        sin[s] = jnp.where(upper, sine, -sine)
    row_in = lax.broadcasted_iota(jnp.int32, (ROWS, WIDTH), 0) + mz * ROWS
    for h in range(HEADS):
        limit[h * ROWS : (h + 1) * ROWS, :] = row_in
    lane = lax.broadcasted_iota(jnp.int32, (8, WIDEST), 1)
    for q in range(4):
        ids = jnp.full((8, WIDEST), BIG, jnp.int32)
        for w in range(2):
            first = away(OFFSETS[q][w]) * ROWS
            for s in range(NSEQ):
                lo = s * PAIR + w * ROWS
                at = lane - lo + first
                here = (lane >= lo) & (lane < lo + ROWS) & (at < counts[s])
                ids = jnp.where(here, at + s * CAP, ids)
        slot[q] = ids

    def ag_copy(i, dr, t):
        sign = 1 - 2 * dr
        far = t == 3
        src = -2 * sign if far else -sign * t
        dst = 4 if far else -sign * (t + 1)
        return remote(
            kv_ring.at[i, 3 + src], kv_ring.at[i, 3 + dst], sem_ag_s.at[i, dr, t], sem_ag_r.at[i, dr, t],
            head=away(2 * sign if far else sign),
        )

    def ag_all(t):
        return [(i, dr) for i in range(2) for dr in range(2) if t < 3 or i == dr]

    for i in range(2):
        own_kv[i].wait()
        for src in others:
            kv_copy(i, src, src).wait_recv()
        for s in range(NSEQ):
            x = kv_got[i, s].astype(F32)
            if i == 0:
                x = rope(x, cos[s], sin[s])
            stage[s * ROWS : (s + 1) * ROWS, :] = x
        kv_ring[i, 3] = stage[...].astype(BF16)
        for dr in range(2):
            ag_copy(i, dr, 0).start()
    for whole in (k_all, v_all):
        for q in range(4):
            whole[q, NSEQ * PAIR : WIDEST, :] = jnp.zeros((WIDEST - NSEQ * PAIR, WIDTH), BF16)

    def place_q(s):
        for h in range(HEADS):
            x = rope(q_got[s, :, h * WIDTH : (h + 1) * WIDTH].astype(F32), cos[s], sin[s])
            stage[h * ROWS : (h + 1) * ROWS, :] = x
        q_all[s] = stage[...].astype(BF16)

    def place_g(s):
        for h in range(HEADS):
            stage[h * ROWS : (h + 1) * ROWS, :] = g_got[s, :, h * WIDTH : (h + 1) * WIDTH].astype(F32)
        g_all[s] = stage[...].astype(BF16)

    def out_copy(send, out, ss, rs, src, to):
        return remote(send.at[to], out.at[:, columns(src, 1024)], ss.at[to], rs.at[src], seq=to)

    o_copy = functools.partial(out_copy, o_send, att_out, sem_o_s, sem_o_r)
    dq_copy = functools.partial(out_copy, dq_send, dq_out, sem_dq_s, sem_dq_r)

    def own_out(send, out, rs):
        return pltpu.make_async_copy(send.at[me], out.at[:, columns(me, 1024)], rs.at[me])

    def send_back(s, own, copy):
        @pl.when(me == s)
        def _():
            own.start()

        @pl.when(me != s)
        def _():
            copy(me, s).start()

    def forward(q):
        for i, whole in ((0, k_all), (1, v_all)):
            for w in range(2):
                x = kv_ring[i, 3 + OFFSETS[q][w]].astype(F32)
                for s in range(NSEQ):
                    pair_stage[s * PAIR + w * ROWS : s * PAIR + (w + 1) * ROWS, :] = x[s * ROWS : (s + 1) * ROWS]
            whole[q, 0 : NSEQ * PAIR, :] = pair_stage[...].astype(BF16)
        for s in reversed(range(NSEQ)):
            lim = limit[...] + s * CAP
            sc = dot_nt(q_all[s], k_all[q, 0 : WIDE[s], :])
            top = jnp.full((CAP, WIDTH), -1e30, F32)
            xs = []
            for lo in range(0, WIDE[s], WIDTH):
                x = jnp.where(slot[q, 0:1, lo : lo + WIDTH] <= lim, sc[:, lo : lo + WIDTH], -1e30)
                top = jnp.maximum(top, x)
                xs.append(x)
            top = jnp.broadcast_to(jnp.max(top, 1, keepdims=True), (CAP, WIDTH))
            if q > 0:
                before = top_all[q - 1, s]
                top = jnp.maximum(top, before)
            top_all[q, s] = top
            total = jnp.zeros((CAP, WIDTH), F32)
            ws = []
            for n, x in enumerate(xs):
                w = jnp.exp2((x - top) * SCALE2)
                w_all[q, :, START[s] + n * WIDTH : START[s] + (n + 1) * WIDTH] = w
                total = total + w
                ws.append(w.astype(BF16))
            acc = dot_nn(jnp.concatenate(ws, 1), v_all[q, 0 : WIDE[s], :])
            if q > 0:
                shrink = jnp.exp2((before - top) * SCALE2)
                total = total + sum_all[s] * shrink
                acc = acc + acc_all[s] * shrink
            if q < 3:
                sum_all[s] = total
                acc_all[s] = acc
            else:
                live = (limit[...] < counts[s]).astype(F32)
                inv = live / jnp.sum(total, 1, keepdims=True)
                inv_all[s] = inv
                att = (acc * inv).astype(BF16)
                att_all[s] = att
                att = att.astype(F32)
                for h in range(HEADS):
                    o_send[s, :, h * WIDTH : (h + 1) * WIDTH] = att[h * ROWS : (h + 1) * ROWS].astype(BF16)
                send_back(s, own_out(o_send, att_out, sem_o_r), o_copy)

    for t in range(4):
        for i, dr in ag_all(t):
            ag_copy(i, dr, t).wait_recv()
            if t < 2:
                ag_copy(i, dr, t + 1).start()
            if t == 1 and i == dr:
                ag_copy(i, dr, 3).start()
        if t == 0:
            own_q.wait()
            for src in others:
                q_copy(src, src).wait_recv()

            def q_step(s, carry):
                place_q(s)
                return carry

            lax.fori_loop(0, NSEQ, q_step, 0)
        forward(t)

    own_g.wait()
    for src in others:
        g_copy(src, src).wait_recv()

    def g_step(s, carry):
        place_g(s)
        delta = jnp.sum(stage[...] * att_all[s].astype(F32), 1, keepdims=True)
        delta_all[s] = jnp.broadcast_to(delta, (CAP, WIDTH))
        return carry

    lax.fori_loop(0, NSEQ, g_step, 0)

    def backward(q):
        for s in reversed(range(NSEQ)):
            width = WIDE[s]
            qb = q_all[s]
            gb = g_all[s]
            delta = delta_all[s]
            scale = inv_all[s]
            if q < 3:
                scale = scale * jnp.exp2((top_all[q, s] - top_all[3, s]) * SCALE2)
            dp = dot_nt(gb, v_all[q, 0:width, :])
            ps, ds = [], []
            for lo in range(0, width, WIDTH):
                p = w_all[q, :, START[s] + lo : START[s] + lo + WIDTH] * scale
                ps.append(p.astype(BF16))
                d = (p * (dp[:, lo : lo + WIDTH] - delta)).astype(BF16)
                ds_all[q, :, START[s] + lo : START[s] + lo + WIDTH] = d
                ds.append(d)
            dv = dot_tn(jnp.concatenate(ps, 1), gb)
            dk = dot_tn(jnp.concatenate(ds, 1), qb)
            if s == NSEQ - 1:
                dv_acc[q] = dv
                dk_acc[q] = dk
            else:
                dv_acc[q, 0:width, :] += dv
                dk_acc[q, 0:width, :] += dk

    accs = (dk_acc, dv_acc)

    def own_part(i, o, s):
        q, w = PLACE[o]
        return accs[i][q, s * PAIR + w * ROWS : s * PAIR + (w + 1) * ROWS, :]

    def rs_copy(kind, dr, i):
        sign = 1 - 2 * dr
        return remote(
            rs_out.at[kind, dr, i], rs_in.at[kind, dr, i], sem_rs_s.at[kind, dr, i], sem_rs_r.at[kind, dr, i],
            head=away(2 * sign if kind == FAR else sign),
        )

    def rs_kinds(kind, dr):
        return [i for i in range(2) if kind != FAR or i == dr]

    def scatter(kind, dr):
        sign = 1 - 2 * dr
        o = 4 if kind == FAR else sign * DISTANCE[kind]
        for i in rs_kinds(kind, dr):
            adds = []
            if kind == SECOND:
                adds = [THIRD] + ([FAR] if i == dr else [])
            elif kind == FIRST:
                adds = [SECOND]
            for a in adds:
                rs_copy(a, dr, i).wait_recv()
            for s in range(NSEQ):
                x = own_part(i, o, s)
                for a in adds:
                    x = x + rs_in[a, dr, i, s].astype(F32)
                rs_out[kind, dr, i, s] = x.astype(BF16)
            rs_copy(kind, dr, i).start()

    backward(3)
    scatter(THIRD, 0)
    scatter(FAR, 0)
    scatter(FAR, 1)
    backward(2)
    scatter(THIRD, 1)
    backward(1)
    backward(0)
    scatter(SECOND, 0)
    scatter(SECOND, 1)

    for s in reversed(range(NSEQ)):
        dq = jnp.zeros((CAP, WIDTH), F32)
        for q in range(4):
            dq = dq + dot_nn(ds_all[q, :, START[s] : START[s] + WIDE[s]], k_all[q, 0 : WIDE[s], :])
        dq = dq * SCALE
        for h in range(HEADS):
            x = rope_t(dq[h * ROWS : (h + 1) * ROWS], cos[s], sin[s])
            dq_send[s, :, h * WIDTH : (h + 1) * WIDTH] = x.astype(BF16)
        send_back(s, own_out(dq_send, dq_out, sem_dq_r), dq_copy)

    scatter(FIRST, 0)
    scatter(FIRST, 1)

    kv_out = (dk_out, dv_out)

    def back_copy(i, src, to):
        return remote(
            kv_send.at[i, to], kv_out[i].at[:, columns(src, WIDTH)], sem_b_s.at[i, to], sem_b_r.at[i, src], seq=to
        )

    own_back = [
        pltpu.make_async_copy(kv_send.at[i, me], kv_out[i].at[:, columns(me, WIDTH)], sem_b_r.at[i, me])
        for i in range(2)
    ]
    for i in range(2):
        for dr in range(2):
            rs_copy(FIRST, dr, i).wait_recv()
        for s in range(NSEQ):
            x = own_part(i, 0, s)
            for dr in range(2):
                x = x + rs_in[FIRST, dr, i, s].astype(F32)
            if i == 0:
                x = rope_t(x * SCALE, cos[s], sin[s])
            kv_send[i, s] = x.astype(BF16)
            send_back(s, own_back[i], functools.partial(back_copy, i))

    own_out(o_send, att_out, sem_o_r).wait()
    own_out(dq_send, dq_out, sem_dq_r).wait()
    for c in own_back:
        c.wait()
    for src in others:
        o_copy(src, me).wait_recv()
        dq_copy(src, me).wait_recv()
        for i in range(2):
            back_copy(i, src, me).wait_recv()
    for to in others:
        for i in range(2):
            kv_copy(i, me, to).wait_send()
            back_copy(i, me, to).wait_send()
        q_copy(me, to).wait_send()
        g_copy(me, to).wait_send()
        o_copy(me, to).wait_send()
        dq_copy(me, to).wait_send()
    for t in range(4):
        for i, dr in ag_all(t):
            ag_copy(i, dr, t).wait_send()
    for kind in range(4):
        for dr in range(2):
            for i in rs_kinds(kind, dr):
                rs_copy(kind, dr, i).wait_send()


def deliver(*refs):
    held, load_sem, store_sem = refs[8:12], refs[12], refs[13]
    loads = [pltpu.make_async_copy(refs[i], held[i], load_sem.at[i]) for i in range(4)]
    stores = [pltpu.make_async_copy(held[i], refs[i + 4], store_sem.at[i]) for i in range(4)]
    for c in loads:
        c.start()
    for i in range(4):
        loads[i].wait()
        stores[i].start()
    for c in stores:
        c.wait()


def shards(queries, routed_keys, routed_values, output_gradient, positions, counts):
    anywhere = pl.BlockSpec(memory_space=pl.ANY)
    dma = pltpu.SemaphoreType.DMA
    out = jax.ShapeDtypeStruct
    wide = (ROWS, QUERY_HEADS * WIDTH)
    slim = (ROWS, GROUPS * WIDTH)
    results = [out(wide, BF16), out(wide, BF16), out(slim, BF16), out(slim, BF16)]
    by_shard = pltpu.VMEM((NSEQ, CAP, WIDTH), F32)
    found = pl.pallas_call(
        kernel,
        out_shape=results,
        in_specs=[anywhere] * 6,
        out_specs=[anywhere] * 4,
        scratch_shapes=[
            pltpu.SMEM((SLOTS,), jnp.int32),
            pltpu.SMEM((NSEQ,), jnp.int32),
            pltpu.VMEM((NSEQ, ROWS, WIDTH), F32),
            pltpu.VMEM((NSEQ, ROWS, WIDTH), F32),
            pltpu.VMEM((NSEQ, ROWS, WIDTH), F32),
            pltpu.VMEM(wide, BF16),
            pltpu.VMEM(wide, BF16),
            pltpu.VMEM(slim, BF16),
            pltpu.VMEM(slim, BF16),
            pltpu.VMEM((NSEQ, ROWS, HEADS * WIDTH), BF16),
            pltpu.VMEM((NSEQ, ROWS, HEADS * WIDTH), BF16),
            pltpu.VMEM((2, NSEQ, ROWS, WIDTH), BF16),
            pltpu.VMEM((2, NZ, CAP, WIDTH), BF16),
            pltpu.VMEM((CAP, WIDTH), F32),
            pltpu.VMEM((NSEQ, CAP, WIDTH), BF16),
            pltpu.VMEM((NSEQ, CAP, WIDTH), BF16),
            pltpu.VMEM((NSEQ * PAIR, WIDTH), F32),
            pltpu.VMEM((4, WIDEST, WIDTH), BF16),
            pltpu.VMEM((4, WIDEST, WIDTH), BF16),
            pltpu.VMEM((4, 8, WIDEST), jnp.int32),
            pltpu.VMEM((CAP, WIDTH), jnp.int32),
            pltpu.VMEM((4, CAP, STORE), F32),
            pltpu.VMEM((4, CAP, STORE), BF16),
            pltpu.VMEM((4, NSEQ, CAP, WIDTH), F32),
            by_shard,
            by_shard,
            by_shard,
            by_shard,
            pltpu.VMEM((NSEQ, CAP, WIDTH), BF16),
            pltpu.VMEM((4, WIDEST, WIDTH), F32),
            pltpu.VMEM((4, WIDEST, WIDTH), F32),
            pltpu.VMEM((NSEQ, ROWS, HEADS * WIDTH), BF16),
            pltpu.VMEM((NSEQ, ROWS, HEADS * WIDTH), BF16),
            pltpu.VMEM((4, 2, 2, NSEQ, ROWS, WIDTH), BF16),
            pltpu.VMEM((4, 2, 2, NSEQ, ROWS, WIDTH), BF16),
            pltpu.VMEM((2, NSEQ, ROWS, WIDTH), BF16),
            dma((2,)), dma((4,)),
            dma((2, NSEQ)), dma((2, NSEQ)), dma((NSEQ,)), dma((NSEQ,)), dma((NSEQ,)), dma((NSEQ,)),
            dma((2, 2, 4)), dma((2, 2, 4)),
            dma((NSEQ,)), dma((NSEQ,)), dma((NSEQ,)), dma((NSEQ,)),
            dma((4, 2, 2)), dma((4, 2, 2)), dma((2, NSEQ)), dma((2, NSEQ)),
        ],
        compiler_params=pltpu.CompilerParams(
            collective_id=0, has_side_effects=True, vmem_limit_bytes=60 * 2**20
        ),
        cost_estimate=pl.CostEstimate(flops=5 * 10**9, bytes_accessed=4 * 10**6, transcendentals=3 * 10**6),
    )(positions, counts, queries, routed_keys, routed_values, output_gradient)
    return pl.pallas_call(
        deliver,
        out_shape=results,
        in_specs=[anywhere] * 4,
        out_specs=[anywhere] * 4,
        scratch_shapes=[
            pltpu.VMEM(wide, BF16), pltpu.VMEM(wide, BF16), pltpu.VMEM(slim, BF16), pltpu.VMEM(slim, BF16),
            dma((4,)), dma((4,)),
        ],
    )(*found)


def solution(mesh):
    rows = P(("dp", "seq", "head"), None)
    return jax.shard_map(
        shards, mesh=mesh, in_specs=(rows, rows, rows, rows, P("dp"), P("dp")), out_specs=(rows,) * 4, check_vma=False
    )
```

time: 84.9 us -> 70.1 us (0.83)
  Pallas kernels: 76.9 us -> 69.2 us
  local copies, waits for them, and re-layouts: 6.22 us -> 0 us
  other arithmetic: 0.89 us -> 0 us
    pallas_call x1 -> x2, Pallas kernels: 76.9 us -> 69.2 us  [the longest x1 67 us: shards(): pl.pallas_call(kernel, out_shape=results, in_specs=[anywhere] * 6, out_sp...]
    unnamed x16 -> x0, local copies, waits for them, and re-layouts: 6.15 us -> none
where the time goes in v2:
time: 70.1 us; the launch traced here: 70 us
  Pallas kernels  69.2 us (99%)
  between operations  0.8 us (1%)
    pallas_call x1, Pallas kernels, shards(): pl.pallas_call(kernel, out_shape=results, in_specs=[anywhere] * 6, out_sp...  67 us
    pallas_call x1, Pallas kernels, shards(): pl.pallas_call(deliver, out_shape=results, in_specs=[anywhere] * 4, out_s...  2.25 us

profile of v2, /device:TPU:1, one launch (start us, length us, event | category | flops | bytes accessed | tf_op | source)
XLA Modules:
  0.0 70.0 jit_solution(14184500277446938550)
XLA Ops:
  0.6 67.0 %shard_map.93 = (bf16[36,8192]{1,0:T(8,128)(2,1)}, bf16[36,8192]{1,0:T(8,128)(2,1)}, bf16[36,1024]{1,0:T(8,128)(2,1)}, bf16[36,1024]{1,0:T(8,128)(2,1)}) custom-call(s32[2304]{0:T(1024)} %pos_in.1, s32[8]{0:T(128)} %counts_in.1, bf16[36,8192]{1,0:T(8,128)(2,1)} %q_in.1, bf16[36,1024]{1,0:T(8,128)(2,1)} %k_in.1, bf16[36,1024]{1,0:T(8,128)(2,1)} %v_in.1, ...), custom_call_target="tpu_custom_call" | custom-call | flops 5000000000 | bytes 4000000 | tf_op jit(solution)/shard_map/pallas_call | solution.py:460
  67.6 2.3 %shard_map.94 = (bf16[36,8192]{1,0:T(8,128)(2,1)}, bf16[36,8192]{1,0:T(8,128)(2,1)}, bf16[36,1024]{1,0:T(8,128)(2,1)}, bf16[36,1024]{1,0:T(8,128)(2,1)}) custom-call(bf16[36,8192]{1,0:T(8,128)(2,1)} %get-tuple-element.8.refs_0_, bf16[36,8192]{1,0:T(8,128)(2,1)} %get-tuple-element.9.refs_1_, bf16[36,1024]{1,0:T(8,128)(2,1)} %get-tuple-element.10.refs_2_, ...), custom_call_target="tpu_custom_call" | custom-call | tf_op jit(solution)/shard_map/pallas_call | solution.py:513

commit v3 on v2

--- a/solution.py
+++ b/solution.py
@@ -17,7 +17,6 @@
 ROWS = 36
 CAP = 288
 SLOTS = 2304
-PAIR = 2 * ROWS
 WIDEST = 640
 ROPE_BASE = 500000.0
 BIG = 1 << 20
@@ -52,11 +51,17 @@
     return x * cos - roll_half(x) * sin
 
 
-OFFSETS = ((0, -1), (1, -2), (2, -3), (3, 4))
-PLACE = {o: (q, w) for q, pair in enumerate(OFFSETS) for w, o in enumerate(pair)}
-WIDE = tuple(-(-PAIR * (s + 1) // WIDTH) * WIDTH for s in range(NSEQ))
-START = tuple(sum(WIDE[:s]) for s in range(NSEQ))
-STORE = sum(WIDE)
+OFFSETS = ((0,), (1, -1), (2, -2), (3, -3), (4,))
+LAST = len(OFFSETS) - 1
+PLACE = {o: (q, w) for q, group in enumerate(OFFSETS) for w, o in enumerate(group)}
+STEP = tuple(ROWS * len(group) for group in OFFSETS)
+WIDE = tuple(tuple(-(-step * (s + 1) // WIDTH) * WIDTH for s in range(NSEQ)) for step in STEP)
+START, STORE = [], 0
+for _wide in WIDE:
+    START.append([])
+    for _w in _wide:
+        START[-1].append(STORE)
+        STORE += _w
 FAR, THIRD, SECOND, FIRST = range(4)
 DISTANCE = (4, 3, 2, 1)
 
@@ -64,8 +69,8 @@
 def kernel(
     pos_in, counts_in, q_in, k_in, v_in, g_in,
     att_out, dq_out, dk_out, dv_out,
-    pos, counts, pos_row, cos, sin, q_own, g_own, k_own, v_own,
-    q_got, g_got, kv_got, kv_ring, stage, q_all, g_all, pair_stage, k_all, v_all,
+    pos, counts, pos_row, cos, sin, q_own, g_own, k_raw, k_own, v_own,
+    q_got, g_got, kv_ring, stage, q_all, g_all, pair_stage, k_all, v_all,
     slot, limit, w_all, ds_all, top_all, sum_all, acc_all, inv_all, delta_all, att_all,
     dk_acc, dv_acc, o_send, dq_send, rs_out, rs_in, kv_send,
     sem_p, sem_in, sem_kv_s, sem_kv_r, sem_q_s, sem_q_r, sem_g_s, sem_g_r, sem_ag_s, sem_ag_r,
@@ -86,7 +91,7 @@
     get_counts = pltpu.make_async_copy(counts_in, counts, sem_p.at[1])
     loads = [
         pltpu.make_async_copy(src, dst, sem_in.at[i])
-        for i, (src, dst) in enumerate(((k_in, k_own), (v_in, v_own), (q_in, q_own), (g_in, g_own)))
+        for i, (src, dst) in enumerate(((k_in, k_raw), (v_in, v_own), (q_in, q_own), (g_in, g_own)))
     ]
     for c in loads:
         c.start()
@@ -105,7 +110,7 @@
 
     def kv_copy(i, src, to):
         return remote(
-            kv_in[i].at[:, columns(to, WIDTH)], kv_got.at[i, src], sem_kv_s.at[i, to], sem_kv_r.at[i, src], seq=to
+            kv_in[i].at[:, columns(to, WIDTH)], kv_ring.at[i, 3, src], sem_kv_s.at[i, to], sem_kv_r.at[i, src], seq=to
         )
 
     def wide_copy(arr, got, ss, rs, src, to):
@@ -115,30 +120,12 @@
     g_copy = functools.partial(wide_copy, g_own, g_got, sem_g_s, sem_g_r)
     others = [lax.rem(me + d, NSEQ) for d in range(1, NSEQ)]
     own_kv = [
-        pltpu.make_async_copy(kv_in[i].at[:, columns(me, WIDTH)], kv_got.at[i, me], sem_kv_r.at[i, me])
+        pltpu.make_async_copy(kv_in[i].at[:, columns(me, WIDTH)], kv_ring.at[i, 3, me], sem_kv_r.at[i, me])
         for i in range(2)
     ]
     own_q = pltpu.make_async_copy(q_own.at[:, columns(me, 1024)], q_got.at[me], sem_q_r.at[me])
     own_g = pltpu.make_async_copy(g_own.at[:, columns(me, 1024)], g_got.at[me], sem_g_r.at[me])
-    pl.semaphore_wait(barrier, NSEQ - 1 + 4)
-    loads[0].wait()
-    loads[1].wait()
-    for to in others:
-        for i in range(2):
-            kv_copy(i, me, to).start()
-    for c in own_kv:
-        c.start()
-    loads[2].wait()
-    for to in others:
-        q_copy(me, to).start()
-    own_q.start()
-    loads[3].wait()
-    for to in others:
-        g_copy(me, to).start()
-    own_g.start()
-
     get_pos.wait()
-    get_counts.wait()
     for s in range(NSEQ):
         for r in range(ROWS):
             at = pos[s * CAP + mz * ROWS + r].astype(F32)
@@ -152,16 +139,34 @@
         cos[s] = jnp.cos(angle)
         sine = jnp.sin(angle)
         sin[s] = jnp.where(upper, sine, -sine)
+    for c in loads:
+        c.wait()
+    for g in range(GROUPS):
+        cols = slice(g * WIDTH, (g + 1) * WIDTH)
+        k_own[:, cols] = rope(k_raw[:, cols].astype(F32), cos[me], sin[me]).astype(BF16)
+    pl.semaphore_wait(barrier, NSEQ - 1 + 4)
+    for i in range(2):
+        for to in others:
+            kv_copy(i, me, to).start()
+        own_kv[i].start()
+    for to in others:
+        q_copy(me, to).start()
+    own_q.start()
+    for to in others:
+        g_copy(me, to).start()
+    own_g.start()
+
+    get_counts.wait()
     row_in = lax.broadcasted_iota(jnp.int32, (ROWS, WIDTH), 0) + mz * ROWS
     for h in range(HEADS):
         limit[h * ROWS : (h + 1) * ROWS, :] = row_in
     lane = lax.broadcasted_iota(jnp.int32, (8, WIDEST), 1)
-    for q in range(4):
+    for q in range(LAST + 1):
         ids = jnp.full((8, WIDEST), BIG, jnp.int32)
-        for w in range(2):
-            first = away(OFFSETS[q][w]) * ROWS
+        for w, o in enumerate(OFFSETS[q]):
+            first = away(o) * ROWS
             for s in range(NSEQ):
-                lo = s * PAIR + w * ROWS
+                lo = s * STEP[q] + w * ROWS
                 at = lane - lo + first
                 here = (lane >= lo) & (lane < lo + ROWS) & (at < counts[s])
                 ids = jnp.where(here, at + s * CAP, ids)
@@ -184,17 +189,12 @@
         own_kv[i].wait()
         for src in others:
             kv_copy(i, src, src).wait_recv()
-        for s in range(NSEQ):
-            x = kv_got[i, s].astype(F32)
-            if i == 0:
-                x = rope(x, cos[s], sin[s])
-            stage[s * ROWS : (s + 1) * ROWS, :] = x
-        kv_ring[i, 3] = stage[...].astype(BF16)
         for dr in range(2):
             ag_copy(i, dr, 0).start()
     for whole in (k_all, v_all):
-        for q in range(4):
-            whole[q, NSEQ * PAIR : WIDEST, :] = jnp.zeros((WIDEST - NSEQ * PAIR, WIDTH), BF16)
+        for q in range(LAST + 1):
+            rest = WIDEST - NSEQ * STEP[q]
+            whole[q, NSEQ * STEP[q] : WIDEST, :] = jnp.zeros((rest, WIDTH), BF16)
 
     def place_q(s):
         for h in range(HEADS):
@@ -216,28 +216,26 @@
     def own_out(send, out, rs):
         return pltpu.make_async_copy(send.at[me], out.at[:, columns(me, 1024)], rs.at[me])
 
-    def send_back(s, own, copy):
-        @pl.when(me == s)
-        def _():
-            own.start()
-
-        @pl.when(me != s)
-        def _():
-            copy(me, s).start()
-
-    def forward(q):
-        for i, whole in ((0, k_all), (1, v_all)):
-            for w in range(2):
-                x = kv_ring[i, 3 + OFFSETS[q][w]].astype(F32)
-                for s in range(NSEQ):
-                    pair_stage[s * PAIR + w * ROWS : s * PAIR + (w + 1) * ROWS, :] = x[s * ROWS : (s + 1) * ROWS]
-            whole[q, 0 : NSEQ * PAIR, :] = pair_stage[...].astype(BF16)
+    def send_back(own, copy):
+        for to in others:
+            copy(me, to).start()
+        own.start()
+
+    def line_up(i, whole, q):
+        for w, o in enumerate(OFFSETS[q]):
+            for s in range(NSEQ):
+                lo = s * STEP[q] + w * ROWS
+                pair_stage[lo : lo + ROWS, :] = kv_ring[i, 3 + o, s].astype(F32)
+        whole[q, 0 : NSEQ * STEP[q], :] = pair_stage[0 : NSEQ * STEP[q], :].astype(BF16)
+
+    def weigh(q):
+        line_up(0, k_all, q)
         for s in reversed(range(NSEQ)):
             lim = limit[...] + s * CAP
-            sc = dot_nt(q_all[s], k_all[q, 0 : WIDE[s], :])
+            sc = dot_nt(q_all[s], k_all[q, 0 : WIDE[q][s], :])
             top = jnp.full((CAP, WIDTH), -1e30, F32)
             xs = []
-            for lo in range(0, WIDE[s], WIDTH):
+            for lo in range(0, WIDE[q][s], WIDTH):
                 x = jnp.where(slot[q, 0:1, lo : lo + WIDTH] <= lim, sc[:, lo : lo + WIDTH], -1e30)
                 top = jnp.maximum(top, x)
                 xs.append(x)
@@ -247,84 +245,102 @@
                 top = jnp.maximum(top, before)
             top_all[q, s] = top
             total = jnp.zeros((CAP, WIDTH), F32)
-            ws = []
             for n, x in enumerate(xs):
                 w = jnp.exp2((x - top) * SCALE2)
-                w_all[q, :, START[s] + n * WIDTH : START[s] + (n + 1) * WIDTH] = w
+                w_all[:, START[q][s] + n * WIDTH : START[q][s] + (n + 1) * WIDTH] = w
                 total = total + w
-                ws.append(w.astype(BF16))
-            acc = dot_nn(jnp.concatenate(ws, 1), v_all[q, 0 : WIDE[s], :])
             if q > 0:
-                shrink = jnp.exp2((before - top) * SCALE2)
-                total = total + sum_all[s] * shrink
-                acc = acc + acc_all[s] * shrink
-            if q < 3:
-                sum_all[s] = total
+                total = total + sum_all[s] * jnp.exp2((before - top) * SCALE2)
+            sum_all[s] = total
+
+    def gather(q):
+        line_up(1, v_all, q)
+        for s in reversed(range(NSEQ)):
+            w = w_all[:, START[q][s] : START[q][s] + WIDE[q][s]].astype(BF16)
+            acc = dot_nn(w, v_all[q, 0 : WIDE[q][s], :])
+            if q > 0:
+                acc = acc + acc_all[s] * jnp.exp2((top_all[q - 1, s] - top_all[q, s]) * SCALE2)
+            if q < LAST:
                 acc_all[s] = acc
             else:
                 live = (limit[...] < counts[s]).astype(F32)
-                inv = live / jnp.sum(total, 1, keepdims=True)
+                inv = live / jnp.sum(sum_all[s], 1, keepdims=True)
                 inv_all[s] = inv
                 att = (acc * inv).astype(BF16)
                 att_all[s] = att
-                att = att.astype(F32)
-                for h in range(HEADS):
-                    o_send[s, :, h * WIDTH : (h + 1) * WIDTH] = att[h * ROWS : (h + 1) * ROWS].astype(BF16)
-                send_back(s, own_out(o_send, att_out, sem_o_r), o_copy)
-
-    for t in range(4):
-        for i, dr in ag_all(t):
-            ag_copy(i, dr, t).wait_recv()
-            if t < 2:
-                ag_copy(i, dr, t + 1).start()
-            if t == 1 and i == dr:
-                ag_copy(i, dr, 3).start()
-        if t == 0:
-            own_q.wait()
-            for src in others:
-                q_copy(src, src).wait_recv()
-
-            def q_step(s, carry):
-                place_q(s)
-                return carry
-
-            lax.fori_loop(0, NSEQ, q_step, 0)
-        forward(t)
+
+    def arrive(t, i):
+        for dr in range(2):
+            if t < 3 or i == dr:
+                ag_copy(i, dr, t).wait_recv()
+                if t < 2:
+                    ag_copy(i, dr, t + 1).start()
+                if t == 1 and i == dr:
+                    ag_copy(i, dr, 3).start()
+
+    def q_step(s, carry):
+        place_q(s)
+        return carry
+
+    arrive(0, 0)
+    arrive(0, 1)
+    own_q.wait()
+    for src in others:
+        q_copy(src, src).wait_recv()
+    lax.fori_loop(0, NSEQ, q_step, 0)
+    weigh(0)
+    gather(0)
+    arrive(1, 0)
+    weigh(1)
+    arrive(1, 1)
+    gather(1)
+    weigh(2)
+    gather(2)
+    arrive(2, 0)
+    weigh(3)
+    arrive(2, 1)
+    gather(3)
+
+    def g_step(s, carry):
+        place_g(s)
+        return carry
 
     own_g.wait()
     for src in others:
         g_copy(src, src).wait_recv()
-
-    def g_step(s, carry):
-        place_g(s)
-        delta = jnp.sum(stage[...] * att_all[s].astype(F32), 1, keepdims=True)
-        delta_all[s] = jnp.broadcast_to(delta, (CAP, WIDTH))
-        return carry
-
     lax.fori_loop(0, NSEQ, g_step, 0)
+    arrive(3, 0)
+    weigh(4)
+    arrive(3, 1)
+    gather(4)
 
     def backward(q):
         for s in reversed(range(NSEQ)):
-            width = WIDE[s]
+            width = WIDE[q][s]
             qb = q_all[s]
             gb = g_all[s]
-            delta = delta_all[s]
             scale = inv_all[s]
-            if q < 3:
-                scale = scale * jnp.exp2((top_all[q, s] - top_all[3, s]) * SCALE2)
+            if q == LAST:
+                delta = jnp.sum(gb.astype(F32) * att_all[s].astype(F32), 1, keepdims=True)
+                delta = jnp.broadcast_to(delta, (CAP, WIDTH))
+                delta_all[s] = delta
+            else:
+                delta = delta_all[s]
+                scale = scale * jnp.exp2((top_all[q, s] - top_all[LAST, s]) * SCALE2)
             dp = dot_nt(gb, v_all[q, 0:width, :])
             ps, ds = [], []
             for lo in range(0, width, WIDTH):
-                p = w_all[q, :, START[s] + lo : START[s] + lo + WIDTH] * scale
+                at = START[q][s] + lo
+                p = w_all[:, at : at + WIDTH] * scale
                 ps.append(p.astype(BF16))
                 d = (p * (dp[:, lo : lo + WIDTH] - delta)).astype(BF16)
-                ds_all[q, :, START[s] + lo : START[s] + lo + WIDTH] = d
+                ds_all[:, at : at + WIDTH] = d
                 ds.append(d)
             dv = dot_tn(jnp.concatenate(ps, 1), gb)
             dk = dot_tn(jnp.concatenate(ds, 1), qb)
             if s == NSEQ - 1:
-                dv_acc[q] = dv
-                dk_acc[q] = dk
+                dv_acc[q, 0:width, :] = dv
+                dk_acc[q, 0:width, :] = dk
             else:
                 dv_acc[q, 0:width, :] += dv
                 dk_acc[q, 0:width, :] += dk
@@ -333,13 +349,14 @@
 
     def own_part(i, o, s):
         q, w = PLACE[o]
-        return accs[i][q, s * PAIR + w * ROWS : s * PAIR + (w + 1) * ROWS, :]
+        lo = s * STEP[q] + w * ROWS
+        return accs[i][q, lo : lo + ROWS, :]
 
     def rs_copy(kind, dr, i):
         sign = 1 - 2 * dr
         return remote(
             rs_out.at[kind, dr, i], rs_in.at[kind, dr, i], sem_rs_s.at[kind, dr, i], sem_rs_r.at[kind, dr, i],
-            head=away(2 * sign if kind == FAR else sign),
+            head=away(2 * sign if kind in (FAR, SECOND) else sign),
         )
 
     def rs_kinds(kind, dr):
@@ -352,8 +369,6 @@
             adds = []
             if kind == SECOND:
                 adds = [THIRD] + ([FAR] if i == dr else [])
-            elif kind == FIRST:
-                adds = [SECOND]
             for a in adds:
                 rs_copy(a, dr, i).wait_recv()
             for s in range(NSEQ):
@@ -363,29 +378,35 @@
                 rs_out[kind, dr, i, s] = x.astype(BF16)
             rs_copy(kind, dr, i).start()
 
+    backward(4)
+    scatter(FAR, 0)
+    scatter(FAR, 1)
+    for s in range(NSEQ):
+        att = att_all[s].astype(F32)
+        for h in range(HEADS):
+            o_send[s, :, h * WIDTH : (h + 1) * WIDTH] = att[h * ROWS : (h + 1) * ROWS].astype(BF16)
+    send_back(own_out(o_send, att_out, sem_o_r), o_copy)
     backward(3)
     scatter(THIRD, 0)
-    scatter(FAR, 0)
-    scatter(FAR, 1)
+    scatter(THIRD, 1)
     backward(2)
-    scatter(THIRD, 1)
     backward(1)
-    backward(0)
+    scatter(FIRST, 0)
+    scatter(FIRST, 1)
     scatter(SECOND, 0)
     scatter(SECOND, 1)
+    backward(0)
 
     for s in reversed(range(NSEQ)):
         dq = jnp.zeros((CAP, WIDTH), F32)
-        for q in range(4):
-            dq = dq + dot_nn(ds_all[q, :, START[s] : START[s] + WIDE[s]], k_all[q, 0 : WIDE[s], :])
+        for q in range(LAST + 1):
+            d = ds_all[:, START[q][s] : START[q][s] + WIDE[q][s]]
+            dq = dq + dot_nn(d, k_all[q, 0 : WIDE[q][s], :])
         dq = dq * SCALE
         for h in range(HEADS):
             x = rope_t(dq[h * ROWS : (h + 1) * ROWS], cos[s], sin[s])
             dq_send[s, :, h * WIDTH : (h + 1) * WIDTH] = x.astype(BF16)
-        send_back(s, own_out(dq_send, dq_out, sem_dq_r), dq_copy)
-
-    scatter(FIRST, 0)
-    scatter(FIRST, 1)
+    send_back(own_out(dq_send, dq_out, sem_dq_r), dq_copy)
 
     kv_out = (dk_out, dv_out)
 
@@ -399,16 +420,17 @@
         for i in range(2)
     ]
     for i in range(2):
-        for dr in range(2):
-            rs_copy(FIRST, dr, i).wait_recv()
+        ends = [(kind, dr) for kind in (FIRST, SECOND) for dr in range(2)]
+        for kind, dr in ends:
+            rs_copy(kind, dr, i).wait_recv()
         for s in range(NSEQ):
             x = own_part(i, 0, s)
-            for dr in range(2):
-                x = x + rs_in[FIRST, dr, i, s].astype(F32)
+            for kind, dr in ends:
+                x = x + rs_in[kind, dr, i, s].astype(F32)
             if i == 0:
                 x = rope_t(x * SCALE, cos[s], sin[s])
             kv_send[i, s] = x.astype(BF16)
-            send_back(s, own_back[i], functools.partial(back_copy, i))
+        send_back(own_back[i], functools.partial(back_copy, i))
 
     own_out(o_send, att_out, sem_o_r).wait()
     own_out(dq_send, dq_out, sem_dq_r).wait()
@@ -472,28 +494,28 @@
             pltpu.VMEM(wide, BF16),
             pltpu.VMEM(slim, BF16),
             pltpu.VMEM(slim, BF16),
+            pltpu.VMEM(slim, BF16),
             pltpu.VMEM((NSEQ, ROWS, HEADS * WIDTH), BF16),
             pltpu.VMEM((NSEQ, ROWS, HEADS * WIDTH), BF16),
-            pltpu.VMEM((2, NSEQ, ROWS, WIDTH), BF16),
-            pltpu.VMEM((2, NZ, CAP, WIDTH), BF16),
+            pltpu.VMEM((2, NZ, NSEQ, ROWS, WIDTH), BF16),
             pltpu.VMEM((CAP, WIDTH), F32),
             pltpu.VMEM((NSEQ, CAP, WIDTH), BF16),
             pltpu.VMEM((NSEQ, CAP, WIDTH), BF16),
-            pltpu.VMEM((NSEQ * PAIR, WIDTH), F32),
-            pltpu.VMEM((4, WIDEST, WIDTH), BF16),
-            pltpu.VMEM((4, WIDEST, WIDTH), BF16),
-            pltpu.VMEM((4, 8, WIDEST), jnp.int32),
+            pltpu.VMEM((NSEQ * max(STEP), WIDTH), F32),
+            pltpu.VMEM((LAST + 1, WIDEST, WIDTH), BF16),
+            pltpu.VMEM((LAST + 1, WIDEST, WIDTH), BF16),
+            pltpu.VMEM((LAST + 1, 8, WIDEST), jnp.int32),
             pltpu.VMEM((CAP, WIDTH), jnp.int32),
-            pltpu.VMEM((4, CAP, STORE), F32),
-            pltpu.VMEM((4, CAP, STORE), BF16),
-            pltpu.VMEM((4, NSEQ, CAP, WIDTH), F32),
+            pltpu.VMEM((CAP, STORE), F32),
+            pltpu.VMEM((CAP, STORE), BF16),
+            pltpu.VMEM((LAST + 1, NSEQ, CAP, WIDTH), F32),
             by_shard,
             by_shard,
             by_shard,
             by_shard,
             pltpu.VMEM((NSEQ, CAP, WIDTH), BF16),
-            pltpu.VMEM((4, WIDEST, WIDTH), F32),
-            pltpu.VMEM((4, WIDEST, WIDTH), F32),
+            pltpu.VMEM((LAST + 1, WIDEST, WIDTH), F32),
+            pltpu.VMEM((LAST + 1, WIDEST, WIDTH), F32),
             pltpu.VMEM((NSEQ, ROWS, HEADS * WIDTH), BF16),
             pltpu.VMEM((NSEQ, ROWS, HEADS * WIDTH), BF16),
             pltpu.VMEM((4, 2, 2, NSEQ, ROWS, WIDTH), BF16),

time: 70.1 us -> 66.8 us (0.953)
  Pallas kernels: 69.2 us -> 65.9 us
    pallas_call x1, Pallas kernels: 67 us -> 63.6 us  [shards(): pl.pallas_call(kernel, out_shape=results, in_specs=[anywhere] * 6, out_sp...]
where the time goes in v3:
time: 66.8 us; the launch traced here: 66.7 us
  Pallas kernels  65.9 us (99%)
  between operations  0.82 us (1%)
    pallas_call x1, Pallas kernels, shards(): pl.pallas_call(kernel, out_shape=results, in_specs=[anywhere] * 6, out_sp...  63.6 us
    pallas_call x1, Pallas kernels, shards(): pl.pallas_call(deliver, out_shape=results, in_specs=[anywhere] * 4, out_s...  2.25 us

profile of v3, /device:TPU:1, one launch (start us, length us, event | category | flops | bytes accessed | tf_op | source)
XLA Modules:
  0.0 66.7 jit_solution(9490743676643490189)
XLA Ops:
  0.6 63.6 %shard_map.93 = (bf16[36,8192]{1,0:T(8,128)(2,1)}, bf16[36,8192]{1,0:T(8,128)(2,1)}, bf16[36,1024]{1,0:T(8,128)(2,1)}, bf16[36,1024]{1,0:T(8,128)(2,1)}) custom-call(s32[2304]{0:T(1024)} %pos_in.1, s32[8]{0:T(128)} %counts_in.1, bf16[36,8192]{1,0:T(8,128)(2,1)} %q_in.1, bf16[36,1024]{1,0:T(8,128)(2,1)} %k_in.1, bf16[36,1024]{1,0:T(8,128)(2,1)} %v_in.1, ...), custom_call_target="tpu_custom_call" | custom-call | flops 5000000000 | bytes 4000000 | tf_op jit(solution)/shard_map/pallas_call | solution.py:482
  64.2 2.3 %shard_map.94 = (bf16[36,8192]{1,0:T(8,128)(2,1)}, bf16[36,8192]{1,0:T(8,128)(2,1)}, bf16[36,1024]{1,0:T(8,128)(2,1)}, bf16[36,1024]{1,0:T(8,128)(2,1)}) custom-call(bf16[36,8192]{1,0:T(8,128)(2,1)} %get-tuple-element.8.refs_0_, bf16[36,8192]{1,0:T(8,128)(2,1)} %get-tuple-element.9.refs_1_, bf16[36,1024]{1,0:T(8,128)(2,1)} %get-tuple-element.10.refs_2_, ...), custom_call_target="tpu_custom_call" | custom-call | tf_op jit(solution)/shard_map/pallas_call | solution.py:535

commit v4 on v3

--- a/solution.py
+++ b/solution.py
@@ -72,7 +72,7 @@
     pos, counts, pos_row, cos, sin, q_own, g_own, k_raw, k_own, v_own,
     q_got, g_got, kv_ring, stage, q_all, g_all, pair_stage, k_all, v_all,
     slot, limit, w_all, ds_all, top_all, sum_all, acc_all, inv_all, delta_all, att_all,
-    dk_acc, dv_acc, o_send, dq_send, rs_out, rs_in, kv_send,
+    dk_acc, dv_acc, dk_turned, dv_turned, o_send, dq_send, rs_out, rs_in, kv_send,
     sem_p, sem_in, sem_kv_s, sem_kv_r, sem_q_s, sem_q_r, sem_g_s, sem_g_r, sem_ag_s, sem_ag_r,
     sem_o_s, sem_o_r, sem_dq_s, sem_dq_r, sem_rs_s, sem_rs_r, sem_b_s, sem_b_r,
 ):
@@ -336,14 +336,17 @@
                 d = (p * (dp[:, lo : lo + WIDTH] - delta)).astype(BF16)
                 ds_all[:, at : at + WIDTH] = d
                 ds.append(d)
-            dv = dot_tn(jnp.concatenate(ps, 1), gb)
-            dk = dot_tn(jnp.concatenate(ds, 1), qb)
+            dv = dot_tn(gb, jnp.concatenate(ps, 1))
+            dk = dot_tn(qb, jnp.concatenate(ds, 1))
             if s == NSEQ - 1:
-                dv_acc[q, 0:width, :] = dv
-                dk_acc[q, 0:width, :] = dk
+                dv_turned[:, 0:width] = dv
+                dk_turned[:, 0:width] = dk
             else:
-                dv_acc[q, 0:width, :] += dv
-                dk_acc[q, 0:width, :] += dk
+                dv_turned[:, 0:width] += dv
+                dk_turned[:, 0:width] += dk
+        width = WIDE[q][NSEQ - 1]
+        dk_acc[q, 0:width, :] = dk_turned[:, 0:width].T
+        dv_acc[q, 0:width, :] = dv_turned[:, 0:width].T
 
     accs = (dk_acc, dv_acc)
 
@@ -362,10 +365,9 @@
     def rs_kinds(kind, dr):
         return [i for i in range(2) if kind != FAR or i == dr]
 
-    def scatter(kind, dr):
-        sign = 1 - 2 * dr
-        o = 4 if kind == FAR else sign * DISTANCE[kind]
-        for i in rs_kinds(kind, dr):
+    def scatter(kind):
+        for i, dr in [(i, dr) for i in range(2) for dr in range(2) if kind != FAR or i == dr]:
+            o = 4 if kind == FAR else (1 - 2 * dr) * DISTANCE[kind]
             adds = []
             if kind == SECOND:
                 adds = [THIRD] + ([FAR] if i == dr else [])
@@ -379,22 +381,18 @@
             rs_copy(kind, dr, i).start()
 
     backward(4)
-    scatter(FAR, 0)
-    scatter(FAR, 1)
+    scatter(FAR)
+    backward(3)
+    scatter(THIRD)
     for s in range(NSEQ):
         att = att_all[s].astype(F32)
         for h in range(HEADS):
             o_send[s, :, h * WIDTH : (h + 1) * WIDTH] = att[h * ROWS : (h + 1) * ROWS].astype(BF16)
     send_back(own_out(o_send, att_out, sem_o_r), o_copy)
-    backward(3)
-    scatter(THIRD, 0)
-    scatter(THIRD, 1)
+    backward(1)
+    scatter(FIRST)
     backward(2)
-    backward(1)
-    scatter(FIRST, 0)
-    scatter(FIRST, 1)
-    scatter(SECOND, 0)
-    scatter(SECOND, 1)
+    scatter(SECOND)
     backward(0)
 
     for s in reversed(range(NSEQ)):
@@ -407,6 +405,23 @@
             x = rope_t(dq[h * ROWS : (h + 1) * ROWS], cos[s], sin[s])
             dq_send[s, :, h * WIDTH : (h + 1) * WIDTH] = x.astype(BF16)
     send_back(own_out(dq_send, dq_out, sem_dq_r), dq_copy)
+
+    for to in others:
+        for i in range(2):
+            kv_copy(i, me, to).wait_send()
+        q_copy(me, to).wait_send()
+        g_copy(me, to).wait_send()
+        o_copy(me, to).wait_send()
+    for t in range(4):
+        for i, dr in ag_all(t):
+            ag_copy(i, dr, t).wait_send()
+    for kind in (FAR, THIRD, FIRST):
+        for dr in range(2):
+            for i in rs_kinds(kind, dr):
+                rs_copy(kind, dr, i).wait_send()
+    own_out(o_send, att_out, sem_o_r).wait()
+    for src in others:
+        o_copy(src, me).wait_recv()
 
     kv_out = (dk_out, dv_out)
 
@@ -432,30 +447,20 @@
             kv_send[i, s] = x.astype(BF16)
         send_back(own_back[i], functools.partial(back_copy, i))
 
-    own_out(o_send, att_out, sem_o_r).wait()
+    for dr in range(2):
+        for i in range(2):
+            rs_copy(SECOND, dr, i).wait_send()
     own_out(dq_send, dq_out, sem_dq_r).wait()
-    for c in own_back:
-        c.wait()
     for src in others:
-        o_copy(src, me).wait_recv()
         dq_copy(src, me).wait_recv()
-        for i in range(2):
+    for to in others:
+        dq_copy(me, to).wait_send()
+    for i in range(2):
+        own_back[i].wait()
+        for src in others:
             back_copy(i, src, me).wait_recv()
-    for to in others:
-        for i in range(2):
-            kv_copy(i, me, to).wait_send()
+        for to in others:
             back_copy(i, me, to).wait_send()
-        q_copy(me, to).wait_send()
-        g_copy(me, to).wait_send()
-        o_copy(me, to).wait_send()
-        dq_copy(me, to).wait_send()
-    for t in range(4):
-        for i, dr in ag_all(t):
-            ag_copy(i, dr, t).wait_send()
-    for kind in range(4):
-        for dr in range(2):
-            for i in rs_kinds(kind, dr):
-                rs_copy(kind, dr, i).wait_send()
 
 
 def deliver(*refs):
@@ -516,6 +521,8 @@
             pltpu.VMEM((NSEQ, CAP, WIDTH), BF16),
             pltpu.VMEM((LAST + 1, WIDEST, WIDTH), F32),
             pltpu.VMEM((LAST + 1, WIDEST, WIDTH), F32),
+            pltpu.VMEM((WIDTH, WIDEST), F32),
+            pltpu.VMEM((WIDTH, WIDEST), F32),
             pltpu.VMEM((NSEQ, ROWS, HEADS * WIDTH), BF16),
             pltpu.VMEM((NSEQ, ROWS, HEADS * WIDTH), BF16),
             pltpu.VMEM((4, 2, 2, NSEQ, ROWS, WIDTH), BF16),

time: 66.8 us -> 64.4 us (0.964)
  Pallas kernels: 65.9 us -> 63.4 us
    pallas_call x1, Pallas kernels: 63.6 us -> 61.2 us  [shards(): pl.pallas_call(kernel, out_shape=results, in_specs=[anywhere] * 6, out_sp...]
where the time goes in v4:
time: 64.4 us; the launch traced here: 64.2 us
  Pallas kernels  63.4 us (98%)
  between operations  0.8 us (1%)
    pallas_call x1, Pallas kernels, shards(): pl.pallas_call(kernel, out_shape=results, in_specs=[anywhere] * 6, out_sp...  61.2 us
    pallas_call x1, Pallas kernels, shards(): pl.pallas_call(deliver, out_shape=results, in_specs=[anywhere] * 4, out_s...  2.25 us

profile of v4, /device:TPU:1, one launch (start us, length us, event | category | flops | bytes accessed | tf_op | source)
XLA Modules:
  0.0 64.2 jit_solution(15759232642552383023)
XLA Ops:
  0.6 61.2 %shard_map.93 = (bf16[36,8192]{1,0:T(8,128)(2,1)}, bf16[36,8192]{1,0:T(8,128)(2,1)}, bf16[36,1024]{1,0:T(8,128)(2,1)}, bf16[36,1024]{1,0:T(8,128)(2,1)}) custom-call(s32[2304]{0:T(1024)} %pos_in.1, s32[8]{0:T(128)} %counts_in.1, bf16[36,8192]{1,0:T(8,128)(2,1)} %q_in.1, bf16[36,1024]{1,0:T(8,128)(2,1)} %k_in.1, bf16[36,1024]{1,0:T(8,128)(2,1)} %v_in.1, ...), custom_call_target="tpu_custom_call" | custom-call | flops 5000000000 | bytes 4000000 | tf_op jit(solution)/shard_map/pallas_call | solution.py:487
  61.8 2.3 %shard_map.94 = (bf16[36,8192]{1,0:T(8,128)(2,1)}, bf16[36,8192]{1,0:T(8,128)(2,1)}, bf16[36,1024]{1,0:T(8,128)(2,1)}, bf16[36,1024]{1,0:T(8,128)(2,1)}) custom-call(bf16[36,8192]{1,0:T(8,128)(2,1)} %get-tuple-element.8.refs_0_, bf16[36,8192]{1,0:T(8,128)(2,1)} %get-tuple-element.9.refs_1_, bf16[36,1024]{1,0:T(8,128)(2,1)} %get-tuple-element.10.refs_2_, ...), custom_call_target="tpu_custom_call" | custom-call | tf_op jit(solution)/shard_map/pallas_call | solution.py:542

commit v5 on v4

--- a/solution.py
+++ b/solution.py
@@ -404,7 +404,16 @@
         for h in range(HEADS):
             x = rope_t(dq[h * ROWS : (h + 1) * ROWS], cos[s], sin[s])
             dq_send[s, :, h * WIDTH : (h + 1) * WIDTH] = x.astype(BF16)
-    send_back(own_out(dq_send, dq_out, sem_dq_r), dq_copy)
+        if s in (6, 4, 2, 0):
+            for to in (s + 1, s):
+
+                @pl.when(me == to)
+                def _():
+                    own_out(dq_send, dq_out, sem_dq_r).start()
+
+                @pl.when(me != to)
+                def _():
+                    dq_copy(me, to).start()
 
     for to in others:
         for i in range(2):

time: 64.4 us -> 63.8 us (level)
  no operation moved by 1% of the time
where the time goes in v5:
time: 63.8 us; the launch traced here: 63.7 us
  Pallas kernels  62.9 us (99%)
  between operations  0.8 us (1%)
    pallas_call x1, Pallas kernels, shards(): pl.pallas_call(kernel, out_shape=results, in_specs=[anywhere] * 6, out_sp...  60.6 us
    pallas_call x1, Pallas kernels, shards(): pl.pallas_call(deliver, out_shape=results, in_specs=[anywhere] * 4, out_s...  2.25 us

profile of v5, /device:TPU:1, one launch (start us, length us, event | category | flops | bytes accessed | tf_op | source)
XLA Modules:
  0.0 63.7 jit_solution(3075434221373114586)
XLA Ops:
  0.6 60.6 %shard_map.93 = (bf16[36,8192]{1,0:T(8,128)(2,1)}, bf16[36,8192]{1,0:T(8,128)(2,1)}, bf16[36,1024]{1,0:T(8,128)(2,1)}, bf16[36,1024]{1,0:T(8,128)(2,1)}) custom-call(s32[2304]{0:T(1024)} %pos_in.1, s32[8]{0:T(128)} %counts_in.1, bf16[36,8192]{1,0:T(8,128)(2,1)} %q_in.1, bf16[36,1024]{1,0:T(8,128)(2,1)} %k_in.1, bf16[36,1024]{1,0:T(8,128)(2,1)} %v_in.1, ...), custom_call_target="tpu_custom_call" | custom-call | flops 5000000000 | bytes 4000000 | tf_op jit(solution)/shard_map/pallas_call | solution.py:496
  61.2 2.3 %shard_map.94 = (bf16[36,8192]{1,0:T(8,128)(2,1)}, bf16[36,8192]{1,0:T(8,128)(2,1)}, bf16[36,1024]{1,0:T(8,128)(2,1)}, bf16[36,1024]{1,0:T(8,128)(2,1)}) custom-call(bf16[36,8192]{1,0:T(8,128)(2,1)} %get-tuple-element.8.refs_0_, bf16[36,8192]{1,0:T(8,128)(2,1)} %get-tuple-element.9.refs_1_, bf16[36,1024]{1,0:T(8,128)(2,1)} %get-tuple-element.10.refs_2_, ...), custom_call_target="tpu_custom_call" | custom-call | tf_op jit(solution)/shard_map/pallas_call | solution.py:551
